TPU v7x, 128 devices: a whole 4x4x4 slice. The times are simulated.
128 devices in a mesh: elem: 128 (over x, y, z, core).
Axes of the slice: x: 4, y: 4, z: 4, core: 2. Of those that a mesh axis runs over, the one named last changes fastest.
Arguments:
- solution: bfloat16 [5, 216, 524288], P(None, None, 'elem'), may hold values from -6 to 6
- wind_field: bfloat16 [3, 216, 524288], P(None, None, 'elem'), may hold values from -6 to 6
- metric_scale: float32 [524288], P('elem'), may hold values from 0.5 to 4
- neighbours: int32 [6, 524288], P(None, 'elem'), may hold values from 0 to 5119
- precursor: bfloat16 [5, 216, 32768], P(None, None, 'elem'), may hold values from -6 to 6
- mortar_send: int32 [128, 2, 1024], P('elem'), may hold values from -1 to 255, as said below
- fringe_table: int32 [3, 65536], P(None, 'elem'), may hold values from 0 to 4095, as said below
- volume_operator_stack: bfloat16 [3, 216, 216], replicated, may hold values from -0.4375 to 0.4375
- surface_lift_weight: bfloat16 [216, 216], replicated, may hold values from -0.4375 to 0.4375
- mortar_proj: bfloat16 [4, 36, 216], replicated, may hold values from -0.4375 to 0.4375
Outputs:
- section_rate: bfloat16 [5, 216, 524288], P(None, None, 'elem')
Inputs may be any that keep to these rules, and one draw needn't show every extreme that they name: `mortar_send`: on partition s, entry [0, d * 8 + c] names the local precursor element that s sends to partition d in its slot c, or -1 where that slot is empty; entry [1, d * 8 + c] is that mortar's type, 0 in empty slots. Every partition receives all 8 slots from at least one partition. `fringe_table`: on partition d, column j: row 0 is the position s * 8 + c of a live slot c that partition s sends to d, distinct within d; row 1 a local element, distinct within d, whose face 0 meets the precursor block; row 2 the mortar type, equal to entry [1, d * 8 + c] of mortar_send on s. `neighbours`: entry [f, e] is the position of the element across face f of local element e in the partition's extended block: below 512 the previous partition's last 512 elements, 512 + i local element i, from 4608 on the next partition's first 512 elements. That element meets face f with its opposite face, nodes aligned.
All inputs are finite; a program needn't handle non-finite values.
Results may differ from a plain program's by a relative error of at most 0.005.
Values may be sent and summed in bfloat16 or wider, within the bound.
No kernel may reach another device: no remote copies, remote signals or barrier semaphores. Data moves between devices by JAX's collectives and lax.ppermute only.
A program may use at most 256 MiB of HBM per device.

v0:
```python
import jax
import jax.numpy as jnp
import numpy as np
from jax import lax
from jax.sharding import PartitionSpec as P

EDGE_NODES = 6
FACE_NODES = 36
MTYPES = 4
BAND = 512


sound_speed = 1.0


def with_halo(block, sides, width):
    for axis, dim in sides:
        count = lax.axis_size(axis)
        forward = [(i, i + 1) for i in range(count - 1)]
        backward = [(target, source) for source, target in forward]
        low = lax.ppermute(
            lax.slice_in_dim(block, block.shape[dim] - width, None, axis=dim), axis, forward
        )
        high = lax.ppermute(lax.slice_in_dim(block, 0, width, axis=dim), axis, backward)
        block = jnp.concatenate([low, block, high], axis=dim)
    return block


def trace_lookup_rows():
    edge = EDGE_NODES
    far_end = edge - 1
    select = np.zeros((6 * edge * edge, edge**3), np.float32)
    for first in range(edge):
        for second in range(edge):
            inner = first * edge + second
            nodes_list = [
                first * edge + second,
                far_end * edge * edge + first * edge + second,
                first * edge * edge + second,
                first * edge * edge + far_end * edge + second,
                first * edge * edge + second * edge,
                first * edge * edge + second * edge + far_end,
            ]
            for face_id in range(6):
                select[face_id * edge * edge + inner, nodes_list[face_id]] = 1.0
    return jnp.asarray(select, dtype=jnp.bfloat16)


def flat_faces(nodal_state_values, trace_picker):
    return jnp.einsum(
        "so,uoq->usq", trace_picker, nodal_state_values, preferred_element_type=jnp.float32
    ).astype(jnp.bfloat16)


def project(blocks, mortar_kinds, mortar_proj):
    projected = jnp.einsum("tqn,vns->vtqs", mortar_proj, blocks, preferred_element_type=jnp.float32)
    selector = (mortar_kinds[None, :] == jnp.arange(MTYPES, dtype=jnp.int32)[:, None]).astype(
        jnp.float32
    )
    return jnp.sum(projected * selector[None, :, None, :], axis=1).astype(jnp.bfloat16)


def local(
    solution,
    wind_field,
    metric_scale,
    neighbours,
    precursor,
    mortar_send,
    fringe_table,
    volume_operator_stack,
    surface_lift_weight,
    mortar_proj,
):
    variables = solution.shape[0]
    elem_count = solution.shape[2]
    trace_picker = trace_lookup_rows()
    flat_traces = flat_faces(solution, trace_picker)
    extended = with_halo(flat_traces, (("elem", 2),), BAND)
    wide_count = extended.shape[2]
    send_index = mortar_send[0, 0]
    live_slot = send_index >= 0
    blocks = jnp.take(precursor, jnp.maximum(send_index, 0), axis=2)
    blocks = jnp.where(live_slot[None, None, :], blocks, jnp.zeros_like(blocks))
    arrived = lax.all_to_all(blocks, "elem", split_axis=2, concat_axis=2, tiled=True)
    chosen = jnp.take(arrived, fringe_table[0], axis=2)
    mortar_trace = project(chosen, fringe_table[2], mortar_proj)
    outer = extended.reshape(variables, 6, FACE_NODES, wide_count)
    face_list = [
        jnp.take(outer[:, face_id ^ 1], neighbours[face_id], axis=2) for face_id in range(6)
    ]
    face_list[0] = face_list[0].at[:, :, fringe_table[1]].set(mortar_trace)
    coupled = jnp.stack(face_list, axis=1).reshape(variables, 6 * FACE_NODES, elem_count)
    wind_faces = (
        flat_faces(wind_field, trace_picker)
        .astype(jnp.float32)
        .reshape(3, 6, FACE_NODES, elem_count)
    )
    speeds = jnp.stack(
        [(2.0 * (face_id % 2) - 1.0) * wind_faces[face_id // 2, face_id] for face_id in range(6)],
        axis=0,
    )
    coefficient = (0.5 * (speeds - jnp.abs(speeds) - sound_speed)).reshape(
        6 * FACE_NODES, elem_count
    )
    surface_term = (
        (flat_traces.astype(jnp.float32) - coupled.astype(jnp.float32)) * coefficient[None]
    ).astype(jnp.bfloat16)
    numerical_flux = (
        wind_field.astype(jnp.float32)[:, None] * solution.astype(jnp.float32)[None]
    ).astype(jnp.bfloat16)
    volume_term = jnp.einsum(
        "phj,pijc->ihc", volume_operator_stack, numerical_flux, preferred_element_type=jnp.float32
    )
    lifted_residual = jnp.einsum(
        "hj,tjy->thy", surface_lift_weight, surface_term, preferred_element_type=jnp.float32
    )
    return (metric_scale[None, None, :] * (lifted_residual - volume_term)).astype(jnp.bfloat16)


def solution(mesh):
    in_specs = (
        P(None, None, "elem"),
        P(None, None, "elem"),
        P("elem"),
        P(None, "elem"),
        P(None, None, "elem"),
        P("elem", None, None),
        P(None, "elem"),
        P(),
        P(),
        P(),
    )
    out_specs = P(None, None, "elem")
    return jax.shard_map(local, mesh=mesh, in_specs=in_specs, out_specs=out_specs, check_vma=False)
```

profile of v0, /device:TPU:6, one launch (start us, length us, event | category | flops | bytes accessed | tf_op | source)
XLA Modules:
  0.0 668.0 jit_solution(16185911700186088470)
XLA Ops:
  54.4 11.7 %reshape.178 = f32[3,6,36,4096]{3,2,1,0:T(8,128)} reshape(f32[3,216,4096]{2,1,0:T(8,128)} %convert_bitcast_fusion) | data formatting | bytes 21233664 | tf_op jit(solution)/shard_map/reshape | solution.py:97
  78.0 12.0 %convert_element_type.62 = f32[5,216,4096]{2,1,0:T(8,128)} convert(bf16[5,216,4096]{2,1,0:T(8,128)(2,1)} %param.13) | non-fusion elementwise | flops 4423680 | bytes 26542080 | tf_op jit(solution)/shard_map/convert_element_type | solution.py:110
  107.1 10.2 %pad_maximum_fusion = bf16[5,216,5120]{2,1,0:T(8,128)(2,1)} fusion(bf16[5,216,512]{2,1,0:T(8,128)(2,1)} %collective-permute-done.1, bf16[5,216,4096]{2,1,0:T(8,128)(2,1)} %copy-done.1, bf16[5,216,512]{2,1,0:T(8,128)(2,1)} %collective-permute-done), kind=kLoop, calls=%fused_computation.17 | loop fusion | flops 33177600 | bytes 22118400 | tf_op jit(solution)/shard_map/concatenate | solution.py:25
  117.3 14.1 %reshape.173 = bf16[5,6,36,5120]{3,2,1,0:T(8,128)(2,1)} reshape(bf16[5,216,5120]{2,1,0:T(8,128)(2,1)} %pad_maximum_fusion) | data formatting | bytes 22118400 | tf_op jit(solution)/shard_map/reshape | solution.py:88
  140.3 10.1 %copy.44 = bf16[5,1,36,5120]{2,0,3,1:T(8,128)(2,1)} copy(bf16[5,1,36,5120]{3,2,1,0:T(8,128)(2,1)} %get-tuple-element.13) | data formatting | bytes 3686400
  150.4 10.1 %copy.45 = bf16[5,1,36,5120]{2,0,3,1:T(8,128)(2,1)} copy(bf16[5,1,36,5120]{3,2,1,0:T(8,128)(2,1)} %get-tuple-element.12) | data formatting | bytes 3686400
  160.5 32.8 %gather_fusion.3 = bf16[4096,5,36]{2,1,0:T(8,128)(2,1)} fusion(bf16[5,36,5120]{1,0,2:T(8,128)(2,1)} %bitcast.114, s32[4096]{0:T(1024)S(1)} %get-tuple-element.28), kind=kCustom, calls=%fused_computation.1.clone | custom fusion | bytes 2965504 | tf_op jit(solution)/shard_map/jit(_take)/gather | solution.py:90
  193.3 16.7 %select_bitcast_fusion.4 = bf16[5,1,36,4096]{2,0,3,1:T(8,128)(2,1)} fusion(bf16[4096,5,36]{2,1,0:T(8,128)(2,1)} %gather_fusion.3, pred[4096]{0:T(1024)(128)(4,1)S(1)} %compare_and_fusion.4), kind=kLoop, calls=%fused_computation.27 | loop fusion | flops 737280 | bytes 2953216 | tf_op jit(solution)/shard_map/stack | solution.py:93
  218.8 10.1 %copy.46 = bf16[5,1,36,5120]{2,0,3,1:T(8,128)(2,1)} copy(bf16[5,1,36,5120]{3,2,1,0:T(8,128)(2,1)} %get-tuple-element.11) | data formatting | bytes 3686400
  228.8 32.8 %gather_fusion.4 = bf16[4096,5,36]{2,1,0:T(8,128)(2,1)} fusion(bf16[5,36,5120]{1,0,2:T(8,128)(2,1)} %bitcast.115, s32[4096]{0:T(1024)S(1)} %get-tuple-element.29), kind=kCustom, calls=%fused_computation.2.clone | custom fusion | bytes 2965504 | tf_op jit(solution)/shard_map/jit(_take)/gather | solution.py:90
  261.7 16.7 %select_bitcast_fusion.3 = bf16[5,1,36,4096]{2,0,3,1:T(8,128)(2,1)} fusion(bf16[4096,5,36]{2,1,0:T(8,128)(2,1)} %gather_fusion.4, pred[4096]{0:T(1024)(128)(4,1)S(1)} %compare_and_fusion.3), kind=kLoop, calls=%fused_computation.26 | loop fusion | flops 737280 | bytes 2953216 | tf_op jit(solution)/shard_map/stack | solution.py:93
  287.1 10.1 %copy.47 = bf16[5,1,36,5120]{2,0,3,1:T(8,128)(2,1)} copy(bf16[5,1,36,5120]{3,2,1,0:T(8,128)(2,1)} %get-tuple-element.10) | data formatting | bytes 3686400
  297.1 32.8 %gather_fusion.5 = bf16[4096,5,36]{2,1,0:T(8,128)(2,1)} fusion(bf16[5,36,5120]{1,0,2:T(8,128)(2,1)} %bitcast.112, s32[4096]{0:T(1024)S(1)} %get-tuple-element.30), kind=kCustom, calls=%fused_computation.3.clone | custom fusion | bytes 2965504 | tf_op jit(solution)/shard_map/jit(_take)/gather | solution.py:90
  330.0 16.7 %select_bitcast_fusion.2 = bf16[5,1,36,4096]{2,0,3,1:T(8,128)(2,1)} fusion(bf16[4096,5,36]{2,1,0:T(8,128)(2,1)} %gather_fusion.5, pred[4096]{0:T(1024)(128)(4,1)S(1)} %compare_and_fusion.2), kind=kLoop, calls=%fused_computation.25 | loop fusion | flops 737280 | bytes 2953216 | tf_op jit(solution)/shard_map/stack | solution.py:93
  365.5 32.8 %gather_fusion.6 = bf16[4096,5,36]{2,1,0:T(8,128)(2,1)} fusion(bf16[5,36,5120]{1,0,2:T(8,128)(2,1)} %bitcast.116, s32[4096]{0:T(1024)S(1)} %get-tuple-element.31), kind=kCustom, calls=%fused_computation.4.clone | custom fusion | bytes 2965504 | tf_op jit(solution)/shard_map/jit(_take)/gather | solution.py:90
  398.3 16.7 %select_bitcast_fusion.1 = bf16[5,1,36,4096]{2,0,3,1:T(8,128)(2,1)} fusion(bf16[4096,5,36]{2,1,0:T(8,128)(2,1)} %gather_fusion.6, pred[4096]{0:T(1024)(128)(4,1)S(1)} %compare_and_fusion.1), kind=kLoop, calls=%fused_computation.24 | loop fusion | flops 737280 | bytes 2953216 | tf_op jit(solution)/shard_map/stack | solution.py:93
  432.2 32.8 %gather_fusion.7 = bf16[4096,5,36]{2,1,0:T(8,128)(2,1)} fusion(bf16[5,36,5120]{1,0,2:T(8,128)(2,1)} %bitcast.113, s32[4096]{0:T(1024)S(1)} %get-tuple-element.32), kind=kCustom, calls=%fused_computation.5.clone | custom fusion | bytes 2965504 | tf_op jit(solution)/shard_map/jit(_take)/gather | solution.py:90
  465.0 16.7 %select_bitcast_fusion = bf16[5,1,36,4096]{2,0,3,1:T(8,128)(2,1)} fusion(bf16[4096,5,36]{2,1,0:T(8,128)(2,1)} %gather_fusion.7, pred[4096]{0:T(1024)(128)(4,1)S(1)} %compare_and_fusion), kind=kLoop, calls=%fused_computation.23 | loop fusion | flops 737280 | bytes 2953216 | tf_op jit(solution)/shard_map/stack | solution.py:93
  490.4 32.8 %gather_fusion.2 = bf16[4096,5,36]{2,1,0:T(8,128)(2,1)} fusion(bf16[5,36,5120]{1,0,2:T(8,128)(2,1)} %bitcast.111, s32[4096]{0:T(1024)S(1)} %get-tuple-element.27), kind=kCustom, calls=%fused_computation.clone | custom fusion | bytes 2965504 | tf_op jit(solution)/shard_map/jit(_take)/gather | solution.py:90
  523.2 16.8 %select_bitcast_fusion.5 = bf16[5,36,4096]{1,0,2:T(8,128)(2,1)} fusion(bf16[4096,5,36]{2,1,0:T(8,128)(2,1)} %gather_fusion.2, pred[4096]{0:T(1024)(128)(4,1)S(1)} %compare_and_fusion.5), kind=kLoop, calls=%fused_computation.28 | loop fusion | flops 737280 | bytes 2953216 | tf_op jit(solution)/shard_map/jit(_take)/select_n | solution.py:90
  546.3 47.5 %scatter_fusion = bf16[5,36,4096]{1,0,2:T(8,128)(2,1)} fusion(bf16[5,36,4096]{1,0,2:T(8,128)(2,1)} %select_bitcast_fusion.5, s32[512]{0:T(512)S(1)} %bitcast.131, bf16[512,5,36]{2,1,0:T(8,128)(2,1)S(1)} %copy.28), kind=kCustom, calls=%fused_computation.8 | custom fusion | bytes 555008 | tf_op jit(solution)/shard_map/scatter | solution.py:92
  613.6 14.3 %reshape.176 = f32[5,216,4096]{2,1,0:T(8,128)} reshape(bf16[5,6,36,4096]{3,2,1,0:T(8,128)(2,1)} %constant_dynamic-update-slice_fusion) | data formatting | bytes 26542080 | tf_op jit(solution)/shard_map/convert_element_type | solution.py:107
  627.9 19.5 %fusion.5 = f32[5,4096,216]{1,2,0:T(8,128)} fusion(f32[5,216,4096]{2,1,0:T(8,128)} %reshape.176, bf16[5,216,4096]{2,1,0:T(8,128)(2,1)} %copy-done.1, f32[216,4096]{1,0:T(8,128)} %fusion.9, bf16[216,216]{1,0:T(8,128)(2,1)S(1)} %copy-done.9), kind=kOutput, calls=%fused_computation.19 | convolution fusion | flops 1928724480 | bytes 47869056 | tf_op jit(solution)/shard_map/hj,tjy->thy/dot_general | solution.py:115
  647.4 20.6 %fusion.6 = bf16[5,216,4096]{2,1,0:T(8,128)(2,1)} fusion(f32[5,4096,216]{1,2,0:T(8,128)} %fusion.5, f32[4096]{0:T(1024)S(1)} %copy-done.8, f32[5,216,4096]{2,1,0:T(8,128)} %convert_element_type.62, f32[3,216,4096]{2,1,0:T(8,128)} %convert_element_type.61, bf16[3,216,216]{2,1,0:T(8,128)(2,1)S(1)} %copy-done), kind=kOutput, calls=%fused_computation.20 | convolution fusion | flops 5772902400 | bytes 55149952 | tf_op jit(solution)/shard_map/phj,pijc->ihc/dot_general | solution.py:112
  (85 shorter events, 180.3 us)
Async XLA Ops:
  0.0 647.4 %copy-start = (bf16[3,216,216]{2,1,0:T(8,128)(2,1)S(1)}, bf16[3,216,216]{2,1,0:T(8,128)(2,1)}, u32[]{:S(2)}) copy-start(bf16[3,216,216]{2,1,0:T(8,128)(2,1)} %param.20) | copy-start | bytes 839812
  0.0 20.9 %copy-start.12 = (s32[1,2,1024]{2,1,0:T(2,128)S(1)}, s32[1,2,1024]{2,1,0:T(2,128)}, u32[]{:S(2)}) copy-start(s32[1,2,1024]{2,1,0:T(2,128)} %param.18) | copy-start | bytes 24580
  0.0 21.0 %copy-start.6 = (bf16[5,216,256]{2,1,0:T(8,128)(2,1)S(1)}, bf16[5,216,256]{2,1,0:T(8,128)(2,1)}, u32[]{:S(2)}) copy-start(bf16[5,216,256]{2,1,0:T(8,128)(2,1)} %param.17) | copy-start | bytes 1658884
  6.2 3.6 copy-start.1
  10.9 96.2 %collective-permute-start = (bf16[5,216,512]{2,1,0:T(8,128)(2,1)}, bf16[5,216,512]{2,1,0:T(8,128)(2,1)}, u32[]{:S(2)}, u32[]{:S(2)}) collective-permute-start(bf16[5,216,512]{2,1,0:T(8,128)(2,1)} %get-tuple-element.14), channel_id=1, source_target_pairs={{0,1},{1,2},{2,3},{3,4},{4,5},{5,6},{6,7},{7,8},{8,9},{9,10},{10,1... | collective-permute-start | bytes 3317768 | tf_op jit(solution)/shard_map/ppermute | solution.py:21
  12.8 94.3 %collective-permute-start.1 = (bf16[5,216,512]{2,1,0:T(8,128)(2,1)S(1)}, bf16[5,216,512]{2,1,0:T(8,128)(2,1)}, u32[]{:S(2)}, u32[]{:S(2)}) collective-permute-start(bf16[5,216,512]{2,1,0:T(8,128)(2,1)S(1)} %get-tuple-element.15), channel_id=1, source_target_pairs={{1,0},{2,1},{3,2},{4,3},{5,4},{6,5},{7,6},{8,7},{9,8},{10,9},{11,1... | collective-permute-start | bytes 3317768 | tf_op jit(solution)/shard_map/ppermute | solution.py:24
  30.1 16.0 %copy-start.11 = (s32[3,512]{1,0:T(4,128)S(1)}, s32[3,512]{1,0:T(4,128)}, u32[]{:S(2)}) copy-start(s32[3,512]{1,0:T(4,128)} %param.19) | copy-start | bytes 18436
  30.1 16.0 %copy-start.10 = (s32[6,4096]{1,0:T(8,128)S(1)}, s32[6,4096]{1,0:T(8,128)}, u32[]{:S(2)}) copy-start(s32[6,4096]{1,0:T(8,128)} %param.16) | copy-start | bytes 294916
  30.1 16.3 %copy-start.7 = (bf16[216,216,1]{1,0,2:T(8,128)(2,1)S(1)}, bf16[216,216,1]{1,0,2:T(8,128)(2,1)}, u32[]{:S(2)}) copy-start(bf16[216,216,1]{1,0,2:T(8,128)(2,1)} %constant.59) | copy-start | bytes 279940
  39.6 500.3 %all-to-all-start = ((bf16[5,216,1024]{1,0,2:T(8,128)(2,1)}), bf16[5,216,1024]{1,0,2:T(8,128)(2,1)}, u32[]{:S(2)}, u32[]{:S(2)}) async-start(bf16[5,216,1024]{1,0,2:T(8,128)(2,1)} %select_bitcast_fusion.6), calls=%async_computation | async-start | bytes 8388608 | tf_op jit(solution)/shard_map/all_to_all | solution.py:85
  523.2 21.7 %copy-start.13 = (bf16[4,36,216]{2,0,1:T(4,128)(2,1)S(1)}, bf16[4,36,216]{2,0,1:T(4,128)(2,1)}, u32[]{:S(2)}) copy-start(bf16[4,36,216]{2,0,1:T(4,128)(2,1)} %param.22) | copy-start | bytes 186628
  545.5 59.9 %copy-start.2 = (bf16[5,1,36,4096]{3,2,1,0:T(8,128)(2,1)S(1)}, bf16[5,1,36,4096]{3,2,1,0:T(8,128)(2,1)}, u32[]{:S(2)}) copy-start(bf16[5,1,36,4096]{3,2,1,0:T(8,128)(2,1)} %copy.35) | copy-start | bytes 4423684
  602.5 7.0 %copy-start.3 = (bf16[5,1,36,4096]{3,2,1,0:T(8,128)(2,1)S(1)}, bf16[5,1,36,4096]{3,2,1,0:T(8,128)(2,1)}, u32[]{:S(2)}) copy-start(bf16[5,1,36,4096]{3,2,1,0:T(8,128)(2,1)} %copy.37) | copy-start | bytes 4423684
  602.5 8.3 %copy-start.4 = (bf16[5,1,36,4096]{3,2,1,0:T(8,128)(2,1)S(1)}, bf16[5,1,36,4096]{3,2,1,0:T(8,128)(2,1)}, u32[]{:S(2)}) copy-start(bf16[5,1,36,4096]{3,2,1,0:T(8,128)(2,1)} %copy.38) | copy-start | bytes 4423684
  602.6 9.7 %copy-start.5 = (bf16[5,1,36,4096]{3,2,1,0:T(8,128)(2,1)S(1)}, bf16[5,1,36,4096]{3,2,1,0:T(8,128)(2,1)}, u32[]{:S(2)}) copy-start(bf16[5,1,36,4096]{3,2,1,0:T(8,128)(2,1)} %copy.39) | copy-start | bytes 4423684
  613.6 14.3 %copy-start.9 = (bf16[216,216]{1,0:T(8,128)(2,1)S(1)}, bf16[216,216]{1,0:T(8,128)(2,1)}, u32[]{:S(2)}) copy-start(bf16[216,216]{1,0:T(8,128)(2,1)} %param.21) | copy-start | bytes 279940
  627.9 19.5 %copy-start.8 = (f32[4096]{0:T(1024)S(1)}, f32[4096]{0:T(1024)}, u32[]{:S(2)}) copy-start(f32[4096]{0:T(1024)} %param.15) | copy-start | bytes 49156
where the time goes:
time: 674 us; the launch traced here: 668 us
  local copies, waits for them, and re-layouts  444 us (66%)
  other arithmetic  152 us (23%)
  matrix products  54.9 us (8%)
  starting transfers between devices  16.5 us (2%)
    gather x6, local copies, waits for them, and re-layouts, local(): jnp.take(outer[:, face_id ^ 1], neighbours[face_id], axis=2)  197 us
    another operation x5, other arithmetic, local(): jnp.stack(face_list, axis=1).reshape(variables, 6 * FACE_NODES, elem_count)  83.5 us
    unnamed x42, local copies, waits for them, and re-layouts  77.1 us
    another operation x7, local copies, waits for them, and re-layouts, local(): jnp.stack(face_list, axis=1).reshape(variables, 6 * FACE_NODES, elem_count)  53.6 us
    scatter x1, local copies, waits for them, and re-layouts, local(): face_list[0] = face_list[0].at[:, :, fringe_table[1]].set(mortar_trace)  47.5 us
    dot_general x1, matrix products, local(): jnp.einsum('phj,pijc->ihc', volume_operator_stack, numerical_flux, prefer...  20.6 us
    dot_general x1, matrix products, local(): jnp.einsum('hj,tjy->thy', surface_lift_weight, surface_term, preferred_el...  19.5 us
    select_n x1, other arithmetic, local(): jnp.take(outer[:, face_id ^ 1], neighbours[face_id], axis=2)  16.8 us
  transfers between devices with their start and end apart: 3, of which 0 were waited for; matrix products, arithmetic and copies ran while one was open for 77% of the time, Pallas kernels for 0%

commit v1 on v0

v1 whole, which is shorter than its diff:
```python
import functools

import jax
import jax.numpy as jnp
import numpy as np
from jax import lax
from jax.experimental import pallas as pl
from jax.experimental.pallas import tpu as pltpu
from jax.sharding import PartitionSpec as P

EDGE = 6
FACES = 6
FACE_NODES = 36
SLOT = 48
LANES = 128
ROW = 2 * LANES
BAND = 512
BLOCK = 256
UNROLL = 32
CAP_KINDS = 4
SOUND_SPEED = 1.0


def face_node_lists():
    grid = np.arange(EDGE**3).reshape(EDGE, EDGE, EDGE)
    end = EDGE - 1
    return [
        grid[0].ravel(),
        grid[end].ravel(),
        grid[:, 0].ravel(),
        grid[:, end].ravel(),
        grid[:, :, 0].ravel(),
        grid[:, :, end].ravel(),
    ]


def face_picker():
    pick = np.zeros((FACES * SLOT, EDGE**3), np.float32)
    for face, nodes in enumerate(face_node_lists()):
        pick[face * SLOT + np.arange(FACE_NODES), nodes] = 1.0
    return jnp.asarray(pick, dtype=jnp.bfloat16)


NT = (((1,), (1,)), ((), ()))


def mortar_kernel(combo_ref, precursor_ref, proj_ref, out_ref):
    variables, _, count = precursor_ref.shape
    slots = combo_ref.shape[0]
    combo = combo_ref[...]
    projected = [
        jnp.dot(proj_ref[...], precursor_ref[v], preferred_element_type=jnp.float32).astype(
            jnp.bfloat16
        )
        for v in range(variables)
    ]
    total = jnp.zeros((slots, ROW), jnp.float32)
    ids = lax.broadcasted_iota(jnp.int32, (slots, count), 1)
    pad = jnp.zeros((ROW - variables * SLOT, count), jnp.bfloat16)
    for kind in range(CAP_KINDS):
        table = jnp.concatenate(
            [item[kind * SLOT : (kind + 1) * SLOT] for item in projected] + [pad], axis=0
        )
        onehot = (combo == ids + kind * count).astype(jnp.float32).astype(jnp.bfloat16)
        total = total + lax.dot_general(onehot, table, NT, preferred_element_type=jnp.float32)
    out_ref[...] = total.astype(jnp.bfloat16)


def mortar_rows(precursor, mortar_send, mortar_proj):
    count = precursor.shape[2]
    combo = jnp.maximum(mortar_send[0, 0], 0) + mortar_send[0, 1] * count
    slots = combo.shape[0]
    proj = jnp.pad(mortar_proj, ((0, 0), (0, SLOT - FACE_NODES), (0, 0)))
    proj = proj.reshape(CAP_KINDS * SLOT, -1)
    return pl.pallas_call(
        mortar_kernel,
        out_shape=jax.ShapeDtypeStruct((slots, ROW), jnp.bfloat16),
        compiler_params=pltpu.CompilerParams(vmem_limit_bytes=32 << 20),
    )(combo[:, None], precursor, proj)


def rate_kernel(
    halo_blocks,
    own_blocks,
    index_hbm,
    fringe_ref,
    low_ref,
    high_ref,
    sol_ref,
    wind_ref,
    metric_ref,
    mortar_ref,
    pick_ref,
    weight_ref,
    eye_ref,
    out_ref,
    rows,
    got,
    operand,
    index,
    sem,
):
    step = pl.program_id(0)
    variables, nodes, _ = sol_ref.shape
    extended_blocks = own_blocks + 2 * halo_blocks
    face_rows = 2 * BLOCK * extended_blocks
    own = own_blocks * BLOCK
    traces = FACES * SLOT

    @pl.when(step == 0)
    def _():
        copy = pltpu.make_async_copy(index_hbm, index, sem)
        copy.start()
        rows[pl.ds(FACES * face_rows, mortar_ref.shape[0]), :] = mortar_ref[...]
        operand[...] = jnp.zeros_like(operand)
        copy.wait()

        def override(j, carry):
            index[fringe_ref[1, j]] = FACES * face_rows + 2 * fringe_ref[0, j]
            return carry

        lax.fori_loop(0, fringe_ref.shape[1], override, 0, unroll=8)

    @pl.when(step < extended_blocks)
    def _():
        before = step < halo_blocks
        after = step >= halo_blocks + own_blocks
        picked = []
        for v in range(variables):
            values = jnp.where(before, low_ref[v], jnp.where(after, high_ref[v], sol_ref[v]))
            picked.append(
                jnp.dot(pick_ref[...], values, preferred_element_type=jnp.float32)
            )
        pad = jnp.zeros((ROW - variables * SLOT, BLOCK), jnp.float32)
        for face in range(FACES):
            block = jnp.concatenate(
                [item[face * SLOT : (face + 1) * SLOT] for item in picked] + [pad], axis=0
            )
            turned = block.T
            start = (face ^ 1) * face_rows + pl.multiple_of(step * 2 * BLOCK, 2 * BLOCK)
            rows[pl.ds(start, BLOCK, stride=2), :] = turned[:, :LANES]
            rows[pl.ds(start + 1, BLOCK, stride=2), :] = turned[:, LANES:]

    @pl.when(step >= extended_blocks)
    def _():
        first = (step - extended_blocks) * BLOCK
        for face in range(FACES):

            def gather(chunk, carry, face=face):
                place = face * own + first + chunk * UNROLL
                held = []
                for u in range(UNROLL):
                    where = pl.multiple_of(index[place + u], 2)
                    held.append(rows[pl.ds(where, 2), :])
                target = face * 2 * BLOCK + pl.multiple_of(chunk * 2 * UNROLL, 2 * UNROLL)
                for u in range(UNROLL):
                    got[pl.ds(target + 2 * u, 2), :] = held[u]
                return carry

            lax.fori_loop(0, BLOCK // UNROLL, gather, 0)

        coupled = []
        coefficient = []
        for face in range(FACES):
            start = face * 2 * BLOCK
            block = jnp.concatenate(
                [
                    got[pl.ds(start, BLOCK, stride=2), :],
                    got[pl.ds(start + 1, BLOCK, stride=2), :],
                ],
                axis=1,
            ).astype(jnp.bfloat16)
            coupled.append(
                lax.dot_general(eye_ref[...], block, NT, preferred_element_type=jnp.float32)
            )
            speed = jnp.dot(
                pick_ref[face * SLOT : (face + 1) * SLOT],
                wind_ref[face // 2],
                preferred_element_type=jnp.float32,
            )
            speed = (2.0 * (face % 2) - 1.0) * speed
            coefficient.append(0.5 * (speed - jnp.abs(speed) - SOUND_SPEED))
        for v in range(variables):
            inside = jnp.dot(pick_ref[...], sol_ref[v], preferred_element_type=jnp.float32)
            for face in range(FACES):
                surface = (
                    inside[face * SLOT : (face + 1) * SLOT]
                    - coupled[face][v * SLOT : (v + 1) * SLOT]
                ) * coefficient[face]
                operand[v, face * SLOT : (face + 1) * SLOT, :] = surface.astype(jnp.bfloat16)
            for a in range(3):
                start = traces + a * (weight_ref.shape[1] - traces) // 3
                operand[v, start : start + nodes, :] = (
                    wind_ref[a].astype(jnp.float32) * sol_ref[v].astype(jnp.float32)
                ).astype(jnp.bfloat16)
            total = jnp.dot(weight_ref[...], operand[v], preferred_element_type=jnp.float32)
            out_ref[v] = (metric_ref[...] * total).astype(jnp.bfloat16)


def section_rate(
    solution, low, high, wind_field, metric_scale, index, fringe, mortar, weight
):
    variables, nodes, own = solution.shape
    own_blocks = own // BLOCK
    halo_blocks = BAND // BLOCK
    extended_blocks = own_blocks + 2 * halo_blocks
    face_rows = 2 * BLOCK * extended_blocks
    depth = weight.shape[1]

    def late(step):
        return jnp.maximum(step - extended_blocks, 0)

    def sol_block(step):
        early = jnp.clip(step - halo_blocks, 0, own_blocks - 1)
        return jnp.where(step < extended_blocks, early, step - extended_blocks)

    whole = pl.BlockSpec(memory_space=pltpu.VMEM)
    return pl.pallas_call(
        functools.partial(rate_kernel, halo_blocks, own_blocks),
        grid=(extended_blocks + own_blocks,),
        in_specs=[
            pl.BlockSpec(memory_space=pl.ANY),
            pl.BlockSpec(memory_space=pltpu.SMEM),
            pl.BlockSpec(
                (variables, nodes, BLOCK), lambda s: (0, 0, jnp.minimum(s, halo_blocks - 1))
            ),
            pl.BlockSpec(
                (variables, nodes, BLOCK),
                lambda s: (0, 0, jnp.clip(s - halo_blocks - own_blocks, 0, halo_blocks - 1)),
            ),
            pl.BlockSpec((variables, nodes, BLOCK), lambda s: (0, 0, sol_block(s))),
            pl.BlockSpec((3, nodes, BLOCK), lambda s: (0, 0, late(s))),
            pl.BlockSpec((1, BLOCK), lambda s: (0, late(s))),
            whole,
            whole,
            whole,
            whole,
        ],
        out_specs=pl.BlockSpec((variables, nodes, BLOCK), lambda s: (0, 0, late(s))),
        out_shape=jax.ShapeDtypeStruct(solution.shape, jnp.bfloat16),
        scratch_shapes=[
            pltpu.VMEM((FACES * face_rows + mortar.shape[0], LANES), jnp.float32),
            pltpu.VMEM((FACES * 2 * BLOCK, LANES), jnp.float32),
            pltpu.VMEM((variables, depth, BLOCK), jnp.bfloat16),
            pltpu.SMEM((FACES * own,), jnp.int32),
            pltpu.SemaphoreType.DMA,
        ],
        compiler_params=pltpu.CompilerParams(vmem_limit_bytes=58 << 20),
    )(
        index,
        fringe,
        low,
        high,
        solution,
        wind_field,
        metric_scale[None],
        mortar,
        face_picker(),
        weight,
        jnp.eye(ROW, dtype=jnp.bfloat16),
    )


def local(
    solution,
    wind_field,
    metric_scale,
    neighbours,
    precursor,
    mortar_send,
    fringe_table,
    volume_operator_stack,
    surface_lift_weight,
    mortar_proj,
):
    _, nodes, own = solution.shape
    count = lax.axis_size("elem")
    sent = mortar_rows(precursor, mortar_send, mortar_proj)
    low = lax.ppermute(solution[:, :, own - BAND :], "elem", [(i, i + 1) for i in range(count - 1)])
    high = lax.ppermute(solution[:, :, :BAND], "elem", [(i + 1, i) for i in range(count - 1)])
    arrived = lax.all_to_all(sent, "elem", split_axis=0, concat_axis=0, tiled=True)
    mortar = arrived.astype(jnp.float32).reshape(-1, LANES)
    offsets = (own + 2 * BAND) * jnp.arange(FACES, dtype=jnp.int32)
    index = (2 * (neighbours + offsets[:, None])).reshape(-1)
    lift = jnp.pad(
        surface_lift_weight.reshape(nodes, FACES, FACE_NODES),
        ((0, 0), (0, 0), (0, SLOT - FACE_NODES)),
    ).reshape(nodes, FACES * SLOT)
    volume = jnp.pad(-volume_operator_stack, ((0, 0), (0, 0), (0, 8)))
    weight = jnp.concatenate([lift] + [volume[a] for a in range(3)], axis=1)
    return section_rate(
        solution, low, high, wind_field, metric_scale, index, fringe_table[:2], mortar, weight
    )


def solution(mesh):
    in_specs = (
        P(None, None, "elem"),
        P(None, None, "elem"),
        P("elem"),
        P(None, "elem"),
        P(None, None, "elem"),
        P("elem", None, None),
        P(None, "elem"),
        P(),
        P(),
        P(),
    )
    out_specs = P(None, None, "elem")
    return jax.shard_map(local, mesh=mesh, in_specs=in_specs, out_specs=out_specs, check_vma=False)
```

time: 674 us -> 126 us (0.19)
  local copies, waits for them, and re-layouts: 444 us -> 6.61 us
  other arithmetic: 152 us -> 2.55 us
  Pallas kernels: 0 us -> 82.7 us
  matrix products: 54.9 us -> 0 us
  waiting for transfers between devices: 0.01 us -> 13.6 us
    gather x8 -> x0, local copies, waits for them, and re-layouts: 208 us -> none  [the longest x6 197 us: local(): jnp.take(outer[:, face_id ^ 1], neighbours[face_id], axis=2)]
    another operation x5 -> x0, other arithmetic: 83.5 us -> none  [local(): jnp.stack(face_list, axis=1).reshape(variables, 6 * FACE_NODES, elem_count)]
    pallas_call x0 -> x2, Pallas kernels: none -> 82.7 us  [the longest x1 80.9 us: section_rate(): pl.pallas_call(functools.partial(rate_kernel, halo_blocks, own_blocks), g...]
    unnamed x42 -> x10, local copies, waits for them, and re-layouts: 77.1 us -> 1.91 us
    another operation x9 -> x0, local copies, waits for them, and re-layouts: 60.4 us -> none  [the longest x7 53.6 us: local(): jnp.stack(face_list, axis=1).reshape(variables, 6 * FACE_NODES, elem_count)]
    dot_general x5 -> x0, matrix products: 54.9 us -> none  [the longest x1 20.6 us: local(): jnp.einsum('phj,pijc->ihc', volume_operator_stack, numerical_flux, prefer...]
    scatter x1 -> x0, local copies, waits for them, and re-layouts: 47.5 us -> none  [local(): face_list[0] = face_list[0].at[:, :, fringe_table[1]].set(mortar_trace)]
    select_n x4 -> x0, other arithmetic: 28 us -> none  [the longest x1 16.8 us: local(): jnp.take(outer[:, face_id ^ 1], neighbours[face_id], axis=2)]
  transfers between devices with their start and end apart: 3 -> 3, of which waited for: 0 -> 2; matrix products, arithmetic and copies ran while one was open for 77% -> 6% of each run, Pallas kernels for 0% -> 0%
where the time goes in v1:
time: 126 us
  Pallas kernels  82.7 us (66%)
  starting transfers between devices  20.2 us (16%)
  waiting for transfers between devices  13.6 us (11%)
  local copies, waits for them, and re-layouts  6.61 us (5%)
  other arithmetic  2.55 us (2%)
    pallas_call x1, Pallas kernels, section_rate(): pl.pallas_call(functools.partial(rate_kernel, halo_blocks, own_blocks), g...  80.9 us
    all_to_all x1, starting transfers between devices, local(): lax.all_to_all(sent, 'elem', split_axis=0, concat_axis=0, tiled=True)  10.5 us
    ppermute x1, waiting for transfers between devices, local(): lax.ppermute(solution[:, :, own - BAND:], 'elem', [(i, i + 1) for i in ra...  8.15 us
    ppermute x1, starting transfers between devices, local(): lax.ppermute(solution[:, :, :BAND], 'elem', [(i + 1, i) for i in range(co...  7.77 us
    ppermute x1, waiting for transfers between devices, local(): lax.ppermute(solution[:, :, :BAND], 'elem', [(i + 1, i) for i in range(co...  5.5 us
  transfers between devices with their start and end apart: 3, of which 2 were waited for; matrix products, arithmetic and copies ran while one was open for 6% of the time, Pallas kernels for 0%

profile of v1, /device:TPU:6, one launch (start us, length us, event | category | flops | bytes accessed | tf_op | source)
XLA Modules:
  0.0 125.8 jit_solution(6094131995864800980)
XLA Ops:
  0.0 0.8 add_bitcast_fusion
  0.8 0.9 copy.17
  1.7 0.2 copy.14.combo_ref
  2.0 1.8 %shard_map.109 = bf16[1024,256]{1,0:T(8,128)(2,1)} custom-call(s32[1024,1]{1,0:T(8,128)S(1)} %copy.14.combo_ref, bf16[5,216,256]{2,1,0:T(8,128)(2,1)S(1)} %copy-done, bf16[192,216]{1,0:T(8,128)(2,1)S(1)} %bitcast.14), custom_call_target="tpu_custom_call" | custom-call | tf_op jit(solution)/shard_map/pallas_call | solution.py:75
  3.7 10.5 %all-to-all-start = ((bf16[128,8,256]{2,1,0:T(8,128)(2,1)}), bf16[128,8,256]{2,1,0:T(8,128)(2,1)S(1)}, u32[]{:S(2)}, u32[]{:S(2)}) async-start(bf16[128,8,256]{2,1,0:T(8,128)(2,1)} %bitcast.3), calls=%async_computation | async-start | bytes 1048576 | tf_op jit(solution)/shard_map/all_to_all | solution.py:281
  14.2 0.0 copy-start.2
  14.2 0.0 copy-start.3
  14.2 1.8 %fusion.4 = (bf16[5,216,512]{2,1,0:T(8,128)(2,1)S(1)}, bf16[5,216,512]{2,1,0:T(8,128)(2,1)S(1)}) fusion(bf16[5,216,4096]{2,1,0:T(8,128)(2,1)} %sol_ref.1), kind=kLoop, calls=%fused_computation.12 | loop fusion | bytes 4423680 | tf_op jit(solution)/shard_map/slice | solution.py:280
  16.1 0.0 copy-start.1
  16.1 7.8 %collective-permute-start.1 = (bf16[5,216,512]{2,1,0:T(8,128)(2,1)S(1)}, bf16[5,216,512]{2,1,0:T(8,128)(2,1)}, u32[]{:S(2)}, u32[]{:S(2)}) collective-permute-start(bf16[5,216,512]{2,1,0:T(8,128)(2,1)S(1)} %get-tuple-element.5), channel_id=1, source_target_pairs={{1,0},{2,1},{3,2},{4,3},{5,4},{6,5},{7,6},{8,7},{9,8},{10,9},{11,1... | collective-permute-start | bytes 3317768 | tf_op jit(solution)/shard_map/ppermute | solution.py:280
  23.8 1.9 %collective-permute-start = (bf16[5,216,512]{2,1,0:T(8,128)(2,1)S(1)}, bf16[5,216,512]{2,1,0:T(8,128)(2,1)}, u32[]{:S(2)}, u32[]{:S(2)}) collective-permute-start(bf16[5,216,512]{2,1,0:T(8,128)(2,1)S(1)} %get-tuple-element.6), channel_id=1, source_target_pairs={{0,1},{1,2},{2,3},{3,4},{4,5},{5,6},{6,7},{7,8},{8,9},{9,10},{10,1... | collective-permute-start | bytes 3317768 | tf_op jit(solution)/shard_map/ppermute | solution.py:279
  25.8 0.1 add_multiply_fusion
  25.9 0.6 slice.24.fringe_ref
  26.5 1.0 copy.15
  27.6 0.1 copy.16
  27.7 0.7 reshape.50.index_hbm
  28.4 0.1 neg.3
  28.5 0.7 fusion.eye_ref
  29.2 1.0 pad_maximum_fusion.weight_ref
  30.2 0.0 all-to-all-done
  30.2 1.1 reshape.54.mortar_ref
  31.3 5.5 %collective-permute-done.1.high_ref = bf16[5,216,512]{2,1,0:T(8,128)(2,1)} collective-permute-done((bf16[5,216,512]{2,1,0:T(8,128)(2,1)S(1)}, bf16[5,216,512]{2,1,0:T(8,128)(2,1)}, u32[]{:S(2)}, u32[]{:S(2)}) %collective-permute-start.1) | collective-permute-done | bytes 1105952 | tf_op jit(solution)/shard_map/ppermute | solution.py:280
  36.8 8.1 %collective-permute-done.low_ref = bf16[5,216,512]{2,1,0:T(8,128)(2,1)} collective-permute-done((bf16[5,216,512]{2,1,0:T(8,128)(2,1)S(1)}, bf16[5,216,512]{2,1,0:T(8,128)(2,1)}, u32[]{:S(2)}, u32[]{:S(2)}) %collective-permute-start) | collective-permute-done | bytes 1105952 | tf_op jit(solution)/shard_map/ppermute | solution.py:279
  44.9 80.9 %shard_map.110 = bf16[5,216,4096]{2,1,0:T(8,128)(2,1)} custom-call(s32[24576]{0:T(1024)} %reshape.50.index_hbm, s32[2,512]{1,0:T(2,128)} %slice.24.fringe_ref, bf16[5,216,512]{2,1,0:T(8,128)(2,1)} %collective-permute-done.low_ref, bf16[5,216,512]{2,1,0:T(8,128)(2,1)} %collective-permute-done.1.high_ref, bf16[5,216,4096]{2,1,0:T(8,128)(2,1)} %sol_ref.1, ...), custom_call_target="tpu_custom_call" | custom-call | tf_op jit(solution)/shard_map/pallas_call | solution.py:218
  (10 shorter events, 0.1 us)
Async XLA Ops:
  0.0 1.9 %copy-start = (bf16[5,216,256]{2,1,0:T(8,128)(2,1)S(1)}, bf16[5,216,256]{2,1,0:T(8,128)(2,1)}, u32[]{:S(2)}) copy-start(bf16[5,216,256]{2,1,0:T(8,128)(2,1)} %precursor_ref.1) | copy-start | bytes 1658884
  3.7 26.4 %all-to-all-start = ((bf16[128,8,256]{2,1,0:T(8,128)(2,1)}), bf16[128,8,256]{2,1,0:T(8,128)(2,1)S(1)}, u32[]{:S(2)}, u32[]{:S(2)}) async-start(bf16[128,8,256]{2,1,0:T(8,128)(2,1)} %bitcast.3), calls=%async_computation | async-start | bytes 1048576 | tf_op jit(solution)/shard_map/all_to_all | solution.py:281
  14.2 11.6 %copy-start.2 = (s32[6,4096]{1,0:T(8,128)S(1)}, s32[6,4096]{1,0:T(8,128)}, u32[]{:S(2)}) copy-start(s32[6,4096]{1,0:T(8,128)} %param.14) | copy-start | bytes 294916
  14.2 11.7 %copy-start.3 = (s32[3,512]{1,0:T(4,128)S(1)}, s32[3,512]{1,0:T(4,128)}, u32[]{:S(2)}) copy-start(s32[3,512]{1,0:T(4,128)} %param.17) | copy-start | bytes 18436
  16.1 12.4 %copy-start.1 = (bf16[3,216,216]{2,1,0:T(8,128)(2,1)S(1)}, bf16[3,216,216]{2,1,0:T(8,128)(2,1)}, u32[]{:S(2)}) copy-start(bf16[3,216,216]{2,1,0:T(8,128)(2,1)} %param.18) | copy-start | bytes 839812
  16.1 20.7 %collective-permute-start.1 = (bf16[5,216,512]{2,1,0:T(8,128)(2,1)S(1)}, bf16[5,216,512]{2,1,0:T(8,128)(2,1)}, u32[]{:S(2)}, u32[]{:S(2)}) collective-permute-start(bf16[5,216,512]{2,1,0:T(8,128)(2,1)S(1)} %get-tuple-element.5), channel_id=1, source_target_pairs={{1,0},{2,1},{3,2},{4,3},{5,4},{6,5},{7,6},{8,7},{9,8},{10,9},{11,1... | collective-permute-start | bytes 3317768 | tf_op jit(solution)/shard_map/ppermute | solution.py:280
  23.8 21.1 %collective-permute-start = (bf16[5,216,512]{2,1,0:T(8,128)(2,1)S(1)}, bf16[5,216,512]{2,1,0:T(8,128)(2,1)}, u32[]{:S(2)}, u32[]{:S(2)}) collective-permute-start(bf16[5,216,512]{2,1,0:T(8,128)(2,1)S(1)} %get-tuple-element.6), channel_id=1, source_target_pairs={{0,1},{1,2},{2,3},{3,4},{4,5},{5,6},{6,7},{7,8},{8,9},{9,10},{10,1... | collective-permute-start | bytes 3317768 | tf_op jit(solution)/shard_map/ppermute | solution.py:279

commit v2 on v0

v2 whole, which is shorter than its diff:
```python
import functools

import jax
import jax.numpy as jnp
import numpy as np
from jax import lax
from jax.experimental import pallas as pl
from jax.experimental.pallas import tpu as pltpu
from jax.sharding import PartitionSpec as P

EDGE = 6
FACES = 6
FACE_NODES = 36
SLOT = 48
TRACES = FACES * SLOT
DEPTH = 224
LANES = 128
ROW = 2 * LANES
BAND = 512
BLOCK = 256
GROUP = 32
FETCH = 1024
KINDS = 4
SOUND_SPEED = 1.0


def face_node_lists():
    grid = np.arange(EDGE**3).reshape(EDGE, EDGE, EDGE)
    end = EDGE - 1
    return [
        grid[0].ravel(),
        grid[end].ravel(),
        grid[:, 0].ravel(),
        grid[:, end].ravel(),
        grid[:, :, 0].ravel(),
        grid[:, :, end].ravel(),
    ]


def outer_nodes():
    return np.unique(np.concatenate(face_node_lists()))


def one_hot_rows(rows, columns, places):
    pick = np.zeros((rows, columns), np.float32)
    for row, column in places:
        pick[row, column] = 1.0
    return jnp.asarray(pick, dtype=jnp.bfloat16)


def face_picker(nodes):
    position = {int(node): place for place, node in enumerate(nodes)}
    places = [
        (face * SLOT + q, position[int(node)])
        for face, held in enumerate(face_node_lists())
        for q, node in enumerate(held)
    ]
    return one_hot_rows(TRACES, len(nodes), places)


def band_kernel(pick_ref, last_ref, first_ref, last_out, first_out):
    for v in range(last_ref.shape[0]):
        for source, target in ((last_ref, last_out), (first_ref, first_out)):
            target[v] = jnp.dot(
                pick_ref[...], source[v], preferred_element_type=jnp.float32
            ).astype(jnp.bfloat16)


def band_nodes(solution):
    variables, nodes, own = solution.shape
    outer = outer_nodes()
    pick = one_hot_rows(len(outer), nodes, list(enumerate(outer)))
    band = jax.ShapeDtypeStruct((variables, len(outer), BAND), jnp.bfloat16)
    return pl.pallas_call(
        band_kernel,
        grid=(1,),
        in_specs=[
            pl.BlockSpec(pick.shape, lambda s: (0, 0)),
            pl.BlockSpec((variables, nodes, BAND), lambda s: (0, 0, own // BAND - 1)),
            pl.BlockSpec((variables, nodes, BAND), lambda s: (0, 0, 0)),
        ],
        out_specs=[pl.BlockSpec(band.shape, lambda s: (0, 0, 0))] * 2,
        out_shape=[band] * 2,
        compiler_params=pltpu.CompilerParams(vmem_limit_bytes=60 << 20),
    )(pick, solution, solution)


def mortar_kernel(
    _, __, send_ref, precursor_ref, proj_ref, lift_ref, volume_ref, out_ref, weight_ref
):
    variables, nodes, count = precursor_ref.shape
    slots = send_ref.shape[2]
    combo = jnp.maximum(send_ref[0, 0:1], 0) + send_ref[0, 1:2] * count
    ids = lax.broadcasted_iota(jnp.int32, (count, slots), 0)
    gap = jnp.zeros((SLOT - FACE_NODES, count), jnp.float32)
    pad = jnp.zeros((ROW - variables * SLOT, count), jnp.bfloat16)
    total = jnp.zeros((ROW, slots), jnp.float32)
    for kind in range(KINDS):
        pieces = []
        for v in range(variables):
            projected = jnp.dot(
                proj_ref[kind], precursor_ref[v], preferred_element_type=jnp.float32
            )
            pieces.append(jnp.concatenate([projected, gap], axis=0).astype(jnp.bfloat16))
        table = jnp.concatenate(pieces + [pad], axis=0)
        onehot = (combo == ids + kind * count).astype(jnp.float32).astype(jnp.bfloat16)
        total = total + jnp.dot(table, onehot, preferred_element_type=jnp.float32)
    out_ref[...] = total.T.astype(jnp.bfloat16)

    width = weight_ref.shape[1]
    row = lax.broadcasted_iota(jnp.int32, (nodes, width), 0)
    column = lax.broadcasted_iota(jnp.int32, (nodes, width), 1)

    def spread(matrix, places):
        place = (column == places).astype(jnp.float32).astype(jnp.bfloat16)
        return jnp.dot(matrix, place, preferred_element_type=jnp.float32)

    weight = spread(lift_ref[...], row + (SLOT - FACE_NODES) * (row // FACE_NODES))
    for a in range(3):
        weight = weight - spread(volume_ref[a], row + TRACES + a * DEPTH)
    weight_ref[...] = weight.astype(jnp.bfloat16)


def mortar_rows(band, index, precursor, mortar_send, mortar_proj, lift, volume):
    nodes = precursor.shape[1]
    whole = pl.BlockSpec(memory_space=pltpu.VMEM)
    return pl.pallas_call(
        mortar_kernel,
        in_specs=[pl.BlockSpec(memory_space=pl.ANY)] * 2 + [whole] * 5,
        out_shape=[
            jax.ShapeDtypeStruct((mortar_send.shape[2], ROW), jnp.bfloat16),
            jax.ShapeDtypeStruct((nodes, TRACES + 3 * DEPTH), jnp.bfloat16),
        ],
        compiler_params=pltpu.CompilerParams(vmem_limit_bytes=60 << 20),
    )(band, index, mortar_send, precursor, mortar_proj, lift, volume)


def rate_kernel(
    index_hbm,
    fringe_ref,
    low_hbm,
    high_hbm,
    sol_hbm,
    wind_ref,
    metric_ref,
    mortar_ref,
    pick_ref,
    pick_outer_ref,
    weight_ref,
    out_ref,
    rows,
    got_even,
    got_odd,
    operand,
    sol,
    halo,
    index,
    sems,
):
    step = pl.program_id(0)
    variables, nodes, own = sol.shape
    face_rows = 2 * (own + 2 * BAND)

    def build(values, pick, block):
        picked = [
            jnp.dot(pick, item, preferred_element_type=jnp.float32).astype(jnp.bfloat16)
            for item in values
        ]
        pad = jnp.zeros((ROW - variables * SLOT, BLOCK), jnp.bfloat16)
        for face in range(FACES):
            turned = jnp.concatenate(
                [item[face * SLOT : (face + 1) * SLOT] for item in picked] + [pad], axis=0
            ).T.astype(jnp.float32)
            start = (face ^ 1) * face_rows + pl.multiple_of(block * 2 * BLOCK, 2 * BLOCK)
            rows[pl.ds(start, BLOCK, stride=2), :] = turned[:, :LANES]
            rows[pl.ds(start + 1, BLOCK, stride=2), :] = turned[:, LANES:]

    def gather_groups(first, got):
        def group(face, chunk):
            places = index.at[pl.ds(face * own + first + chunk * GROUP, GROUP)]
            held = [rows[pl.ds(pl.multiple_of(places[u], 2), 2), :] for u in range(GROUP)]
            target = 2 * (face * BLOCK + chunk * GROUP)
            for u in range(GROUP):
                got[target + 2 * u : target + 2 * u + 2, :] = held[u]

        for face in range(FACES):
            for chunk in range(BLOCK // GROUP):
                yield group(face, chunk)

    def emit(groups, count):
        for _ in range(count):
            next(groups, None)

    def compute(part, got, groups):
        inner = slice(part * BLOCK, (part + 1) * BLOCK)
        block = pl.ds(pl.multiple_of((2 * step + part) * BLOCK, BLOCK), BLOCK)
        coupled = []
        coefficient = []
        for face in range(FACES):
            start = face * 2 * BLOCK
            fetched = jnp.concatenate(
                [
                    got[pl.ds(start, BLOCK, stride=2), :],
                    got[pl.ds(start + 1, BLOCK, stride=2), :],
                ],
                axis=1,
            ).astype(jnp.bfloat16)
            coupled.append(fetched.T)
            speed = jnp.dot(
                pick_ref[face * SLOT : (face + 1) * SLOT],
                wind_ref[face // 2, :, inner],
                preferred_element_type=jnp.float32,
            )
            emit(groups, 1)
            speed = (2.0 * (face % 2) - 1.0) * speed
            coefficient.append(0.5 * (speed - jnp.abs(speed) - SOUND_SPEED))
            emit(groups, 1)
        for v in range(variables):
            values = sol[v, :, block]
            inside = jnp.dot(pick_ref[...], values, preferred_element_type=jnp.float32)
            emit(groups, 1)
            for face in range(FACES):
                surface = (
                    inside[face * SLOT : (face + 1) * SLOT]
                    - coupled[face][v * SLOT : (v + 1) * SLOT].astype(jnp.float32)
                ) * coefficient[face]
                operand[v, face * SLOT : (face + 1) * SLOT, :] = surface.astype(jnp.bfloat16)
                if face % 2:
                    emit(groups, 1)
            for a in range(3):
                start = TRACES + a * DEPTH
                operand[v, start : start + nodes, :] = wind_ref[a, :, inner] * values
                emit(groups, 1)
            total = jnp.dot(weight_ref[...], operand[v], preferred_element_type=jnp.float32)
            out_ref[v, :, inner] = (metric_ref[:, inner] * total).astype(jnp.bfloat16)
        for _ in groups:
            pass

    @pl.when(step == 0)
    def _():
        fetches = [
            pltpu.make_async_copy(
                sol_hbm.at[:, :, c * FETCH : (c + 1) * FETCH],
                sol.at[:, :, c * FETCH : (c + 1) * FETCH],
                sems.at[c],
            )
            for c in range(own // FETCH)
        ]
        last = own // FETCH
        index_copy = pltpu.make_async_copy(index_hbm, index, sems.at[last])
        low_copy = pltpu.make_async_copy(low_hbm, halo.at[0], sems.at[last + 1])
        high_copy = pltpu.make_async_copy(high_hbm, halo.at[1], sems.at[last + 2])
        index_copy.start()
        for copy in fetches:
            copy.start()
        low_copy.start()
        high_copy.start()

        operand[...] = jnp.zeros_like(operand)
        slots = mortar_ref.shape[0]
        mortar = mortar_ref[...].astype(jnp.float32)
        rows[pl.ds(FACES * face_rows, slots, stride=2), :] = mortar[:, :LANES]
        rows[pl.ds(FACES * face_rows + 1, slots, stride=2), :] = mortar[:, LANES:]
        index_copy.wait()

        def override(j, carry):
            index[fringe_ref[1, j]] = FACES * face_rows + 2 * fringe_ref[0, j]
            return carry

        lax.fori_loop(0, fringe_ref.shape[1], override, 0, unroll=8)

        for c, copy in enumerate(fetches):
            copy.wait()

            def build_own(i, carry, c=c):
                block = c * (FETCH // BLOCK) + i
                lanes = pl.ds(pl.multiple_of(block * BLOCK, BLOCK), BLOCK)
                build(
                    [sol[v, :, lanes] for v in range(variables)],
                    pick_ref[...],
                    block + BAND // BLOCK,
                )
                return carry

            lax.fori_loop(0, FETCH // BLOCK, build_own, 0, unroll=2)
        low_copy.wait()
        high_copy.wait()
        for side, first in ((0, 0), (1, (BAND + own) // BLOCK)):

            def build_halo(i, carry, side=side, first=first):
                lanes = pl.ds(pl.multiple_of(i * BLOCK, BLOCK), BLOCK)
                build(
                    [halo[side, v, :, lanes] for v in range(variables)],
                    pick_outer_ref[...],
                    first + i,
                )
                return carry

            lax.fori_loop(0, BAND // BLOCK, build_halo, 0, unroll=2)
        for _ in gather_groups(0, got_even):
            pass

    first = 2 * step * BLOCK
    compute(0, got_even, gather_groups(first + BLOCK, got_odd))
    following = jnp.minimum(first + 2 * BLOCK, own - BLOCK)
    compute(1, got_odd, gather_groups(following, got_even))


FACE_EMIT = 2
VAR_EMIT = 7


def section_rate(
    solution, low, high, wind_field, metric_scale, index, fringe, mortar, weight
):
    variables, nodes, own = solution.shape
    face_rows = 2 * (own + 2 * BAND)
    depth = weight.shape[1]
    outer = outer_nodes()
    width = 2 * BLOCK
    whole = pl.BlockSpec(memory_space=pltpu.VMEM)
    anywhere = pl.BlockSpec(memory_space=pl.ANY)
    return pl.pallas_call(
        rate_kernel,
        grid=(own // width,),
        in_specs=[
            anywhere,
            pl.BlockSpec(memory_space=pltpu.SMEM),
            anywhere,
            anywhere,
            anywhere,
            pl.BlockSpec((3, nodes, width), lambda s: (0, 0, s)),
            pl.BlockSpec((1, width), lambda s: (0, s)),
            whole,
            whole,
            whole,
            whole,
        ],
        out_specs=pl.BlockSpec((variables, nodes, width), lambda s: (0, 0, s)),
        out_shape=jax.ShapeDtypeStruct(solution.shape, jnp.bfloat16),
        scratch_shapes=[
            pltpu.VMEM((FACES * face_rows + 2 * mortar.shape[0], LANES), jnp.float32),
            pltpu.VMEM((FACES * 2 * BLOCK, LANES), jnp.float32),
            pltpu.VMEM((FACES * 2 * BLOCK, LANES), jnp.float32),
            pltpu.VMEM((variables, depth, BLOCK), jnp.bfloat16),
            pltpu.VMEM(solution.shape, jnp.bfloat16),
            pltpu.VMEM((2,) + low.shape, jnp.bfloat16),
            pltpu.SMEM((FACES * own,), jnp.int32),
            pltpu.SemaphoreType.DMA((own // FETCH + 3,)),
        ],
        compiler_params=pltpu.CompilerParams(vmem_limit_bytes=62 << 20),
    )(
        index,
        fringe,
        low,
        high,
        solution,
        wind_field,
        metric_scale[None],
        mortar,
        face_picker(np.arange(nodes)),
        face_picker(outer),
        weight,
    )


def local(
    solution,
    wind_field,
    metric_scale,
    neighbours,
    precursor,
    mortar_send,
    fringe_table,
    volume_operator_stack,
    surface_lift_weight,
    mortar_proj,
):
    own = solution.shape[2]
    count = lax.axis_size("elem")
    last, first = band_nodes(solution)
    low = lax.ppermute(last, "elem", [(i, i + 1) for i in range(count - 1)])
    high = lax.ppermute(first, "elem", [(i + 1, i) for i in range(count - 1)])
    offsets = (own + 2 * BAND) * jnp.arange(FACES, dtype=jnp.int32)
    index = (2 * (neighbours + offsets[:, None])).reshape(-1)
    sent, weight = mortar_rows(
        last,
        index,
        precursor,
        mortar_send,
        mortar_proj,
        surface_lift_weight,
        volume_operator_stack,
    )
    mortar = lax.all_to_all(sent, "elem", split_axis=0, concat_axis=0, tiled=True)
    return section_rate(
        solution, low, high, wind_field, metric_scale, index, fringe_table, mortar, weight
    )


def solution(mesh):
    in_specs = (
        P(None, None, "elem"),
        P(None, None, "elem"),
        P("elem"),
        P(None, "elem"),
        P(None, None, "elem"),
        P("elem", None, None),
        P(None, "elem"),
        P(),
        P(),
        P(),
    )
    out_specs = P(None, None, "elem")
    return jax.shard_map(local, mesh=mesh, in_specs=in_specs, out_specs=out_specs, check_vma=False)
```

time: 674 us -> 96.7 us (0.14)
  the two profiles are of different devices: /device:TPU:6 before, /device:TPU:1 now
where the time goes in v2:
time: 96.7 us; the launch traced here: 96.5 us
  Pallas kernels  59.4 us (61%)
  blocking collectives  27.5 us (28%)
  starting transfers between devices  6.84 us (7%)
  local copies, waits for them, and re-layouts  2.45 us (3%)
    pallas_call x1, Pallas kernels, section_rate(): pl.pallas_call(rate_kernel, grid=(own // width,), in_specs=[anywhere, pl....  52.1 us
    all_to_all x1, blocking collectives, local(): lax.all_to_all(sent, 'elem', split_axis=0, concat_axis=0, tiled=True)  27.5 us
    pallas_call x1, Pallas kernels, mortar_rows(): pl.pallas_call(mortar_kernel, in_specs=[pl.BlockSpec(memory_space=pl.ANY)...  3.92 us
    ppermute x1, starting transfers between devices, local(): low = lax.ppermute(last, 'elem', [(i, i + 1) for i in range(count - 1)])  3.52 us
    pallas_call x1, Pallas kernels, band_nodes(): pl.pallas_call(band_kernel, grid=(1,), in_specs=[pl.BlockSpec(pick.shape,...  3.33 us
    ppermute x1, starting transfers between devices, local(): high = lax.ppermute(first, 'elem', [(i + 1, i) for i in range(count - 1)])  3.32 us
  transfers between devices with their start and end apart: 2, of which 0 were waited for; matrix products, arithmetic and copies ran while one was open for 1% of the time, Pallas kernels for 4%

profile of v2, /device:TPU:1, one launch (start us, length us, event | category | flops | bytes accessed | tf_op | source)
XLA Modules:
  0.0 96.5 jit_solution(14665209119124984253)
XLA Ops:
  0.0 0.0 copy-start.2
  0.0 0.0 copy-start.3
  0.0 3.3 %shard_map.127 = (bf16[5,152,512]{2,1,0:T(8,128)(2,1)}, bf16[5,152,512]{2,1,0:T(8,128)(2,1)}) custom-call(bf16[152,216]{1,0:T(8,128)(2,1)} %constant.10.clone.pick_ref, bf16[5,216,4096]{2,1,0:T(8,128)(2,1)} %sol_hbm.1, bf16[5,216,4096]{2,1,0:T(8,128)(2,1)} %sol_hbm.1), custom_call_target="tpu_custom_call" | custom-call | tf_op jit(solution)/shard_map/pallas_call | solution.py:74
  3.3 3.3 %collective-permute-start.1 = (bf16[5,152,512]{2,1,0:T(8,128)(2,1)}, bf16[5,152,512]{2,1,0:T(8,128)(2,1)S(1)}, u32[]{:S(2)}, u32[]{:S(2)}) collective-permute-start(bf16[5,152,512]{2,1,0:T(8,128)(2,1)} %get-tuple-element.10), channel_id=1, source_target_pairs={{1,0},{2,1},{3,2},{4,3},{5,4},{6,5},{7,6},{8,7},{9,8},{10,9},{11,1... | collective-permute-start | bytes 2334728 | tf_op jit(solution)/shard_map/ppermute | solution.py:383
  6.7 3.5 %collective-permute-start = (bf16[5,152,512]{2,1,0:T(8,128)(2,1)}, bf16[5,152,512]{2,1,0:T(8,128)(2,1)S(1)}, u32[]{:S(2)}, u32[]{:S(2)}) collective-permute-start(bf16[5,152,512]{2,1,0:T(8,128)(2,1)} %get-tuple-element.9._), channel_id=1, source_target_pairs={{0,1},{1,2},{2,3},{3,4},{4,5},{5,6},{6,7},{7,8},{8,9},{9,10},{10,1... | collective-permute-start | bytes 2334728 | tf_op jit(solution)/shard_map/ppermute | solution.py:382
  10.2 0.0 copy-done.2
  10.2 0.1 add_multiply_fusion
  10.3 0.0 copy-done.3
  10.3 0.6 copy.14.proj_ref
  10.9 0.7 reshape.9.__.index_hbm
  11.6 3.9 %shard_map.128 = (bf16[1024,256]{1,0:T(8,128)(2,1)}, bf16[216,960]{1,0:T(8,128)(2,1)}) custom-call(bf16[5,152,512]{2,1,0:T(8,128)(2,1)} %get-tuple-element.9._, s32[24576]{0:T(1024)} %reshape.9.__.index_hbm, s32[1,2,1024]{2,1,0:T(2,128)} %send_ref.1, bf16[5,216,256]{2,1,0:T(8,128)(2,1)} %precursor_ref.1, bf16[4,36,216]{2,1,0:T(8,128)(2,1)} %copy.14.proj_ref, ...), custom_call_target="tpu_custom_call" | custom-call | tf_op jit(solution)/shard_map/pallas_call | solution.py:127
  15.6 27.5 %all_to_all.11 = bf16[128,8,256]{2,1,0:T(8,128)(2,1)} all-to-all(bf16[128,8,256]{2,1,0:T(8,128)(2,1)} %bitcast.4), channel_id=1, replica_groups=mesh['elem'=128] {'elem'}, dimensions={0} | all-to-all | bytes 1048576 | tf_op jit(solution)/shard_map/all_to_all | solution.py:395
  43.0 0.0 collective-permute-done.1.high_hbm
  43.0 0.0 copy-start
  43.0 0.0 collective-permute-done.low_hbm
  43.0 0.0 copy-start.1
  43.0 0.9 copy-done
  43.9 0.2 copy-done.1
  44.2 52.1 %shard_map.129 = bf16[5,216,4096]{2,1,0:T(8,128)(2,1)} custom-call(s32[24576]{0:T(1024)} %reshape.9.__.index_hbm, s32[3,512]{1,0:T(4,128)} %fringe_ref.1, bf16[5,152,512]{2,1,0:T(8,128)(2,1)} %copy-done.1, bf16[5,152,512]{2,1,0:T(8,128)(2,1)} %copy-done, bf16[5,216,4096]{2,1,0:T(8,128)(2,1)} %sol_hbm.1, bf16[3,216,4096]{2,1,0:T(8,128)(2,1)} %wind_ref.1, ...), custom_call_target="tpu_custom_call" | custom-call | tf_op jit(solution)/shard_map/pallas_call | solution.py:323
  (1 shorter events, 0.0 us)
Async XLA Ops:
  0.0 10.2 %copy-start.2 = (s32[6,4096]{1,0:T(8,128)S(1)}, s32[6,4096]{1,0:T(8,128)}, u32[]{:S(2)}) copy-start(s32[6,4096]{1,0:T(8,128)} %param.16) | copy-start | bytes 294916
  0.0 10.3 %copy-start.3 = (bf16[4,36,216]{2,0,1:T(4,128)(2,1)S(1)}, bf16[4,36,216]{2,0,1:T(4,128)(2,1)}, u32[]{:S(2)}) copy-start(bf16[4,36,216]{2,0,1:T(4,128)(2,1)} %param.22) | copy-start | bytes 186628
  3.3 39.7 %collective-permute-start.1 = (bf16[5,152,512]{2,1,0:T(8,128)(2,1)}, bf16[5,152,512]{2,1,0:T(8,128)(2,1)S(1)}, u32[]{:S(2)}, u32[]{:S(2)}) collective-permute-start(bf16[5,152,512]{2,1,0:T(8,128)(2,1)} %get-tuple-element.10), channel_id=1, source_target_pairs={{1,0},{2,1},{3,2},{4,3},{5,4},{6,5},{7,6},{8,7},{9,8},{10,9},{11,1... | collective-permute-start | bytes 2334728 | tf_op jit(solution)/shard_map/ppermute | solution.py:383
  6.7 36.4 %collective-permute-start = (bf16[5,152,512]{2,1,0:T(8,128)(2,1)}, bf16[5,152,512]{2,1,0:T(8,128)(2,1)S(1)}, u32[]{:S(2)}, u32[]{:S(2)}) collective-permute-start(bf16[5,152,512]{2,1,0:T(8,128)(2,1)} %get-tuple-element.9._), channel_id=1, source_target_pairs={{0,1},{1,2},{2,3},{3,4},{4,5},{5,6},{6,7},{7,8},{8,9},{9,10},{10,1... | collective-permute-start | bytes 2334728 | tf_op jit(solution)/shard_map/ppermute | solution.py:382
  43.0 0.9 copy-start
  43.0 1.1 %copy-start.1 = (bf16[5,152,512]{2,1,0:T(8,128)(2,1)}, bf16[5,152,512]{2,1,0:T(8,128)(2,1)S(1)}, u32[]{:S(2)}) copy-start(bf16[5,152,512]{2,1,0:T(8,128)(2,1)S(1)} %collective-permute-done.low_hbm) | copy-start | bytes 2334724

commit v3 on v2

--- a/solution.py
+++ b/solution.py
@@ -12,8 +12,7 @@
 FACES = 6
 FACE_NODES = 36
 SLOT = 48
-TRACES = FACES * SLOT
-DEPTH = 224
+TIGHT = 40
 LANES = 128
 ROW = 2 * LANES
 BAND = 512
@@ -48,17 +47,17 @@
     return jnp.asarray(pick, dtype=jnp.bfloat16)
 
 
-def face_picker(nodes):
+def face_picker(nodes, slot):
     position = {int(node): place for place, node in enumerate(nodes)}
     places = [
-        (face * SLOT + q, position[int(node)])
+        (face * slot + q, position[int(node)])
         for face, held in enumerate(face_node_lists())
         for q, node in enumerate(held)
     ]
-    return one_hot_rows(TRACES, len(nodes), places)
-
-
-def band_kernel(pick_ref, last_ref, first_ref, last_out, first_out):
+    return one_hot_rows(FACES * slot, len(nodes), places)
+
+
+def band_kernel(_, pick_ref, last_ref, first_ref, last_out, first_out):
     for v in range(last_ref.shape[0]):
         for source, target in ((last_ref, last_out), (first_ref, first_out)):
             target[v] = jnp.dot(
@@ -66,7 +65,7 @@
             ).astype(jnp.bfloat16)
 
 
-def band_nodes(solution):
+def band_nodes(after, solution):
     variables, nodes, own = solution.shape
     outer = outer_nodes()
     pick = one_hot_rows(len(outer), nodes, list(enumerate(outer)))
@@ -75,6 +74,7 @@
         band_kernel,
         grid=(1,),
         in_specs=[
+            pl.BlockSpec(memory_space=pl.ANY),
             pl.BlockSpec(pick.shape, lambda s: (0, 0)),
             pl.BlockSpec((variables, nodes, BAND), lambda s: (0, 0, own // BAND - 1)),
             pl.BlockSpec((variables, nodes, BAND), lambda s: (0, 0, 0)),
@@ -82,11 +82,11 @@
         out_specs=[pl.BlockSpec(band.shape, lambda s: (0, 0, 0))] * 2,
         out_shape=[band] * 2,
         compiler_params=pltpu.CompilerParams(vmem_limit_bytes=60 << 20),
-    )(pick, solution, solution)
+    )(after, pick, solution, solution)
 
 
 def mortar_kernel(
-    _, __, send_ref, precursor_ref, proj_ref, lift_ref, volume_ref, out_ref, weight_ref
+    send_ref, precursor_ref, proj_ref, lift_ref, out_ref, weight_ref
 ):
     variables, nodes, count = precursor_ref.shape
     slots = send_ref.shape[2]
@@ -111,28 +111,74 @@
     row = lax.broadcasted_iota(jnp.int32, (nodes, width), 0)
     column = lax.broadcasted_iota(jnp.int32, (nodes, width), 1)
 
-    def spread(matrix, places):
-        place = (column == places).astype(jnp.float32).astype(jnp.bfloat16)
-        return jnp.dot(matrix, place, preferred_element_type=jnp.float32)
-
-    weight = spread(lift_ref[...], row + (SLOT - FACE_NODES) * (row // FACE_NODES))
-    for a in range(3):
-        weight = weight - spread(volume_ref[a], row + TRACES + a * DEPTH)
-    weight_ref[...] = weight.astype(jnp.bfloat16)
-
-
-def mortar_rows(band, index, precursor, mortar_send, mortar_proj, lift, volume):
+    places = row + (TIGHT - FACE_NODES) * (row // FACE_NODES)
+    place = (column == places).astype(jnp.float32).astype(jnp.bfloat16)
+    weight_ref[...] = jnp.dot(
+        lift_ref[...], place, preferred_element_type=jnp.float32
+    ).astype(jnp.bfloat16)
+
+
+def mortar_rows(precursor, mortar_send, mortar_proj, lift):
     nodes = precursor.shape[1]
     whole = pl.BlockSpec(memory_space=pltpu.VMEM)
     return pl.pallas_call(
         mortar_kernel,
-        in_specs=[pl.BlockSpec(memory_space=pl.ANY)] * 2 + [whole] * 5,
+        in_specs=[whole] * 4,
         out_shape=[
             jax.ShapeDtypeStruct((mortar_send.shape[2], ROW), jnp.bfloat16),
-            jax.ShapeDtypeStruct((nodes, TRACES + 3 * DEPTH), jnp.bfloat16),
+            jax.ShapeDtypeStruct((nodes, FACES * TIGHT), jnp.bfloat16),
         ],
         compiler_params=pltpu.CompilerParams(vmem_limit_bytes=60 << 20),
-    )(band, index, mortar_send, precursor, mortar_proj, lift, volume)
+    )(mortar_send, precursor, mortar_proj, lift)
+
+
+def volume_kernel(_, sol_ref, wind_ref, pick_ref, operator_ref, volume_ref, speed_ref):
+    for face in range(FACES):
+        speed = jnp.dot(
+            pick_ref[face * SLOT : (face + 1) * SLOT],
+            wind_ref[face // 2],
+            preferred_element_type=jnp.float32,
+        )
+        speed_ref[face * SLOT : (face + 1) * SLOT] = (
+            (2.0 * (face % 2) - 1.0) * speed
+        ).astype(jnp.bfloat16)
+    for v in range(sol_ref.shape[0]):
+        parts = [
+            jnp.dot(operator_ref[a], wind_ref[a] * sol_ref[v], preferred_element_type=jnp.float32)
+            for a in range(3)
+        ]
+        volume_ref[v] = parts[0] + parts[1] + parts[2]
+
+
+def volume_terms(band, solution, wind_field, operators):
+    variables, nodes, own = solution.shape
+    width = 2 * BLOCK
+    whole = pl.BlockSpec(memory_space=pltpu.VMEM)
+    return pl.pallas_call(
+        volume_kernel,
+        grid=(own // width,),
+        in_specs=[
+            pl.BlockSpec(memory_space=pl.ANY),
+            pl.BlockSpec((variables, nodes, width), lambda s: (0, 0, s)),
+            pl.BlockSpec((3, nodes, width), lambda s: (0, 0, s)),
+            whole,
+            whole,
+        ],
+        out_specs=[
+            pl.BlockSpec((variables, nodes, width), lambda s: (0, 0, s)),
+            pl.BlockSpec((FACES * SLOT, width), lambda s: (0, s)),
+        ],
+        out_shape=[
+            jax.ShapeDtypeStruct(solution.shape, jnp.float32),
+            jax.ShapeDtypeStruct((FACES * SLOT, own), jnp.bfloat16),
+        ],
+        cost_estimate=pl.CostEstimate(
+            flops=6 * variables * nodes * nodes * own,
+            bytes_accessed=40 * nodes * own,
+            transcendentals=0,
+        ),
+        compiler_params=pltpu.CompilerParams(vmem_limit_bytes=60 << 20),
+    )(band, solution, wind_field, face_picker(np.arange(nodes), SLOT), operators)
 
 
 def rate_kernel(
@@ -141,17 +187,18 @@
     low_hbm,
     high_hbm,
     sol_hbm,
-    wind_ref,
+    volume_ref,
+    speed_ref,
     metric_ref,
     mortar_ref,
     pick_ref,
     pick_outer_ref,
+    pick_tight_ref,
     weight_ref,
     out_ref,
     rows,
     got_even,
     got_odd,
-    operand,
     sol,
     halo,
     index,
@@ -206,33 +253,24 @@
                 axis=1,
             ).astype(jnp.bfloat16)
             coupled.append(fetched.T)
-            speed = jnp.dot(
-                pick_ref[face * SLOT : (face + 1) * SLOT],
-                wind_ref[face // 2, :, inner],
-                preferred_element_type=jnp.float32,
+            speed = speed_ref[face * SLOT : (face + 1) * SLOT, inner].astype(jnp.float32)[:TIGHT]
+            coefficient.append(0.5 * (speed - jnp.abs(speed) - SOUND_SPEED))
+            emit(groups, 3)
+        for v in range(variables):
+            inside = jnp.dot(
+                pick_tight_ref[...], sol[v, :, block], preferred_element_type=jnp.float32
             )
-            emit(groups, 1)
-            speed = (2.0 * (face % 2) - 1.0) * speed
-            coefficient.append(0.5 * (speed - jnp.abs(speed) - SOUND_SPEED))
-            emit(groups, 1)
-        for v in range(variables):
-            values = sol[v, :, block]
-            inside = jnp.dot(pick_ref[...], values, preferred_element_type=jnp.float32)
-            emit(groups, 1)
+            pieces = []
             for face in range(FACES):
-                surface = (
-                    inside[face * SLOT : (face + 1) * SLOT]
-                    - coupled[face][v * SLOT : (v + 1) * SLOT].astype(jnp.float32)
-                ) * coefficient[face]
-                operand[v, face * SLOT : (face + 1) * SLOT, :] = surface.astype(jnp.bfloat16)
-                if face % 2:
-                    emit(groups, 1)
-            for a in range(3):
-                start = TRACES + a * DEPTH
-                operand[v, start : start + nodes, :] = wind_ref[a, :, inner] * values
+                beyond = coupled[face][v * SLOT : (v + 1) * SLOT].astype(jnp.float32)[:TIGHT]
+                tight = slice(face * TIGHT, (face + 1) * TIGHT)
+                pieces.append((inside[tight] - beyond) * coefficient[face])
                 emit(groups, 1)
-            total = jnp.dot(weight_ref[...], operand[v], preferred_element_type=jnp.float32)
-            out_ref[v, :, inner] = (metric_ref[:, inner] * total).astype(jnp.bfloat16)
+            surface = jnp.concatenate(pieces, axis=0).astype(jnp.bfloat16)
+            total = jnp.dot(weight_ref[...], surface, preferred_element_type=jnp.float32)
+            out_ref[v, :, inner] = (
+                metric_ref[:, inner] * (total - volume_ref[v, :, inner])
+            ).astype(jnp.bfloat16)
         for _ in groups:
             pass
 
@@ -256,7 +294,6 @@
         low_copy.start()
         high_copy.start()
 
-        operand[...] = jnp.zeros_like(operand)
         slots = mortar_ref.shape[0]
         mortar = mortar_ref[...].astype(jnp.float32)
         rows[pl.ds(FACES * face_rows, slots, stride=2), :] = mortar[:, :LANES]
@@ -302,20 +339,18 @@
 
     first = 2 * step * BLOCK
     compute(0, got_even, gather_groups(first + BLOCK, got_odd))
-    following = jnp.minimum(first + 2 * BLOCK, own - BLOCK)
-    compute(1, got_odd, gather_groups(following, got_even))
-
-
-FACE_EMIT = 2
-VAR_EMIT = 7
+
+    @pl.when(step >= 0)
+    def _():
+        following = jnp.minimum(first + 2 * BLOCK, own - BLOCK)
+        compute(1, got_odd, gather_groups(following, got_even))
 
 
 def section_rate(
-    solution, low, high, wind_field, metric_scale, index, fringe, mortar, weight
+    solution, low, high, volume, speed, metric_scale, index, fringe, mortar, weight
 ):
     variables, nodes, own = solution.shape
     face_rows = 2 * (own + 2 * BAND)
-    depth = weight.shape[1]
     outer = outer_nodes()
     width = 2 * BLOCK
     whole = pl.BlockSpec(memory_space=pltpu.VMEM)
@@ -329,8 +364,10 @@
             anywhere,
             anywhere,
             anywhere,
-            pl.BlockSpec((3, nodes, width), lambda s: (0, 0, s)),
+            pl.BlockSpec((variables, nodes, width), lambda s: (0, 0, s)),
+            pl.BlockSpec((FACES * SLOT, width), lambda s: (0, s)),
             pl.BlockSpec((1, width), lambda s: (0, s)),
+            whole,
             whole,
             whole,
             whole,
@@ -342,7 +379,6 @@
             pltpu.VMEM((FACES * face_rows + 2 * mortar.shape[0], LANES), jnp.float32),
             pltpu.VMEM((FACES * 2 * BLOCK, LANES), jnp.float32),
             pltpu.VMEM((FACES * 2 * BLOCK, LANES), jnp.float32),
-            pltpu.VMEM((variables, depth, BLOCK), jnp.bfloat16),
             pltpu.VMEM(solution.shape, jnp.bfloat16),
             pltpu.VMEM((2,) + low.shape, jnp.bfloat16),
             pltpu.SMEM((FACES * own,), jnp.int32),
@@ -355,11 +391,13 @@
         low,
         high,
         solution,
-        wind_field,
+        volume,
+        speed,
         metric_scale[None],
         mortar,
-        face_picker(np.arange(nodes)),
-        face_picker(outer),
+        face_picker(np.arange(nodes), SLOT),
+        face_picker(outer, SLOT),
+        face_picker(np.arange(nodes), TIGHT),
         weight,
     )
 
@@ -378,23 +416,25 @@
 ):
     own = solution.shape[2]
     count = lax.axis_size("elem")
-    last, first = band_nodes(solution)
+    sent, weight = mortar_rows(precursor, mortar_send, mortar_proj, surface_lift_weight)
+    mortar = lax.all_to_all(sent, "elem", split_axis=0, concat_axis=0, tiled=True)
+    last, first = band_nodes(sent, solution)
     low = lax.ppermute(last, "elem", [(i, i + 1) for i in range(count - 1)])
     high = lax.ppermute(first, "elem", [(i + 1, i) for i in range(count - 1)])
+    volume, speed = volume_terms(last, solution, wind_field, volume_operator_stack)
     offsets = (own + 2 * BAND) * jnp.arange(FACES, dtype=jnp.int32)
     index = (2 * (neighbours + offsets[:, None])).reshape(-1)
-    sent, weight = mortar_rows(
-        last,
+    return section_rate(
+        solution,
+        low,
+        high,
+        volume,
+        speed,
+        metric_scale,
         index,
-        precursor,
-        mortar_send,
-        mortar_proj,
-        surface_lift_weight,
-        volume_operator_stack,
-    )
-    mortar = lax.all_to_all(sent, "elem", split_axis=0, concat_axis=0, tiled=True)
-    return section_rate(
-        solution, low, high, wind_field, metric_scale, index, fringe_table, mortar, weight
+        fringe_table,
+        mortar,
+        weight,
     )
 
 

time: 96.7 us -> 94.6 us (0.978)
  the two profiles are of different devices: /device:TPU:1 before, /device:TPU:6 now
where the time goes in v3:
time: 94.6 us; the launch traced here: 94.2 us
  Pallas kernels  70.8 us (75%)
  starting transfers between devices  20 us (21%)
  local copies, waits for them, and re-layouts  3.27 us (3%)
    pallas_call x1, Pallas kernels, section_rate(): pl.pallas_call(rate_kernel, grid=(own // width,), in_specs=[anywhere, pl....  46.6 us
    pallas_call x1, Pallas kernels, volume_terms(): pl.pallas_call(volume_kernel, grid=(own // width,), in_specs=[pl.BlockSpe...  17.5 us
    all_to_all x1, starting transfers between devices, local(): lax.all_to_all(sent, 'elem', split_axis=0, concat_axis=0, tiled=True)  10.5 us
    ppermute x1, starting transfers between devices, local(): high = lax.ppermute(first, 'elem', [(i + 1, i) for i in range(count - 1)])  7.62 us
    pallas_call x1, Pallas kernels, band_nodes(): pl.pallas_call(band_kernel, grid=(1,), in_specs=[pl.BlockSpec(memory_spac...  3.36 us
    pallas_call x1, Pallas kernels, mortar_rows(): pl.pallas_call(mortar_kernel, in_specs=[whole] * 4, out_shape=[jax.ShapeD...  3.25 us
    unnamed x7, local copies, waits for them, and re-layouts  2.58 us
    ppermute x1, starting transfers between devices, local(): low = lax.ppermute(last, 'elem', [(i, i + 1) for i in range(count - 1)])  1.92 us
  transfers between devices with their start and end apart: 3, of which 0 were waited for; matrix products, arithmetic and copies ran while one was open for 1% of the time, Pallas kernels for 22%

profile of v3, /device:TPU:6, one launch (start us, length us, event | category | flops | bytes accessed | tf_op | source)
XLA Modules:
  0.0 94.2 jit_solution(881916644944478280)
XLA Ops:
  0.0 1.5 %copy.16.proj_ref = bf16[4,36,216]{2,1,0:T(8,128)(2,1)} copy(bf16[4,36,216]{2,0,1:T(4,128)(2,1)} %param.24) | data formatting | bytes 124416 | tf_op args[9]
  1.5 3.3 %shard_map.145 = (bf16[1024,256]{1,0:T(8,128)(2,1)}, bf16[216,240]{1,0:T(8,128)(2,1)}) custom-call(s32[1,2,1024]{2,1,0:T(2,128)} %send_ref.1, bf16[5,216,256]{2,1,0:T(8,128)(2,1)} %precursor_ref.1, bf16[4,36,216]{2,1,0:T(8,128)(2,1)} %copy.16.proj_ref, bf16[216,216]{1,0:T(8,128)(2,1)} %lift_ref.1), custom_call_target="tpu_custom_call" | custom-call | tf_op jit(solution)/shard_map/pallas_call | solution.py:124
  4.8 10.5 %all-to-all-start = ((bf16[128,8,256]{2,1,0:T(8,128)(2,1)}), bf16[128,8,256]{2,1,0:T(8,128)(2,1)S(1)}, u32[]{:S(2)}, u32[]{:S(2)}) async-start(bf16[128,8,256]{2,1,0:T(8,128)(2,1)} %bitcast.4), calls=%async_computation | async-start | bytes 1048576 | tf_op jit(solution)/shard_map/all_to_all | solution.py:420
  15.3 0.0 copy-start.2
  15.3 3.4 %shard_map.146 = (bf16[5,152,512]{2,1,0:T(8,128)(2,1)}, bf16[5,152,512]{2,1,0:T(8,128)(2,1)}) custom-call(bf16[1024,256]{1,0:T(8,128)(2,1)} %get-tuple-element.11._, bf16[152,216]{1,0:T(8,128)(2,1)} %constant.12.clone.pick_ref, bf16[5,216,4096]{2,1,0:T(8,128)(2,1)} %sol_hbm.1, bf16[5,216,4096]{2,1,0:T(8,128)(2,1)} %sol_hbm.1), custom_call_target="tpu_custom_call" | custom-call | tf_op jit(solution)/shard_map/pallas_call | solution.py:73
  18.6 7.6 %collective-permute-start.1 = (bf16[5,152,512]{2,1,0:T(8,128)(2,1)}, bf16[5,152,512]{2,1,0:T(8,128)(2,1)S(1)}, u32[]{:S(2)}, u32[]{:S(2)}) collective-permute-start(bf16[5,152,512]{2,1,0:T(8,128)(2,1)} %get-tuple-element.13), channel_id=1, source_target_pairs={{1,0},{2,1},{3,2},{4,3},{5,4},{6,5},{7,6},{8,7},{9,8},{10,9},{11,1... | collective-permute-start | bytes 2334728 | tf_op jit(solution)/shard_map/ppermute | solution.py:423
  26.3 1.9 %collective-permute-start = (bf16[5,152,512]{2,1,0:T(8,128)(2,1)}, bf16[5,152,512]{2,1,0:T(8,128)(2,1)}, u32[]{:S(2)}, u32[]{:S(2)}) collective-permute-start(bf16[5,152,512]{2,1,0:T(8,128)(2,1)} %get-tuple-element.12._), channel_id=1, source_target_pairs={{0,1},{1,2},{2,3},{3,4},{4,5},{5,6},{6,7},{7,8},{8,9},{9,10},{10,1... | collective-permute-start | bytes 2334728 | tf_op jit(solution)/shard_map/ppermute | solution.py:422
  28.2 0.0 copy-done.2
  28.2 0.1 add_multiply_fusion
  28.3 0.7 reshape.9.index_hbm
  29.0 17.5 %shard_map.147 = (f32[5,216,4096]{2,1,0:T(8,128)}, bf16[288,4096]{1,0:T(8,128)(2,1)}) custom-call(bf16[5,152,512]{2,1,0:T(8,128)(2,1)} %get-tuple-element.12._, bf16[5,216,4096]{2,1,0:T(8,128)(2,1)} %sol_hbm.1, bf16[3,216,4096]{2,1,0:T(8,128)(2,1)} %wind_ref.1, bf16[288,216]{1,0:T(8,128)(2,1)} %constant.13.clone.pick_ref, bf16[3,216,216]{2,1,0:T(8,128)(2,1)} %operator_ref.1), custom_call_target="tpu_custom_call" | custom-call | flops 5733089280 | bytes 35389440 | tf_op jit(solution)/shard_map/pallas_call | solution.py:157
  46.5 0.0 all-to-all-done
  46.5 0.0 copy-start
  46.5 0.0 collective-permute-done.1.high_hbm
  46.5 0.0 copy-start.1
  46.5 0.0 collective-permute-done.low_hbm
  46.5 0.8 copy-done
  47.3 0.3 copy-done.1
  47.6 46.6 %shard_map.148 = bf16[5,216,4096]{2,1,0:T(8,128)(2,1)} custom-call(s32[24576]{0:T(1024)} %reshape.9.index_hbm, s32[3,512]{1,0:T(4,128)} %fringe_ref.1, bf16[5,152,512]{2,1,0:T(8,128)(2,1)} %collective-permute-done.low_hbm, bf16[5,152,512]{2,1,0:T(8,128)(2,1)} %copy-done.1, bf16[5,216,4096]{2,1,0:T(8,128)(2,1)} %sol_hbm.1, ...), custom_call_target="tpu_custom_call" | custom-call | tf_op jit(solution)/shard_map/pallas_call | solution.py:358
  (1 shorter events, 0.0 us)
Async XLA Ops:
  4.8 41.7 %all-to-all-start = ((bf16[128,8,256]{2,1,0:T(8,128)(2,1)}), bf16[128,8,256]{2,1,0:T(8,128)(2,1)S(1)}, u32[]{:S(2)}, u32[]{:S(2)}) async-start(bf16[128,8,256]{2,1,0:T(8,128)(2,1)} %bitcast.4), calls=%async_computation | async-start | bytes 1048576 | tf_op jit(solution)/shard_map/all_to_all | solution.py:420
  15.3 12.9 %copy-start.2 = (s32[6,4096]{1,0:T(8,128)S(1)}, s32[6,4096]{1,0:T(8,128)}, u32[]{:S(2)}) copy-start(s32[6,4096]{1,0:T(8,128)} %param.18) | copy-start | bytes 294916
  18.6 27.9 %collective-permute-start.1 = (bf16[5,152,512]{2,1,0:T(8,128)(2,1)}, bf16[5,152,512]{2,1,0:T(8,128)(2,1)S(1)}, u32[]{:S(2)}, u32[]{:S(2)}) collective-permute-start(bf16[5,152,512]{2,1,0:T(8,128)(2,1)} %get-tuple-element.13), channel_id=1, source_target_pairs={{1,0},{2,1},{3,2},{4,3},{5,4},{6,5},{7,6},{8,7},{9,8},{10,9},{11,1... | collective-permute-start | bytes 2334728 | tf_op jit(solution)/shard_map/ppermute | solution.py:423
  26.3 20.3 %collective-permute-start = (bf16[5,152,512]{2,1,0:T(8,128)(2,1)}, bf16[5,152,512]{2,1,0:T(8,128)(2,1)}, u32[]{:S(2)}, u32[]{:S(2)}) collective-permute-start(bf16[5,152,512]{2,1,0:T(8,128)(2,1)} %get-tuple-element.12._), channel_id=1, source_target_pairs={{0,1},{1,2},{2,3},{3,4},{4,5},{5,6},{6,7},{7,8},{8,9},{9,10},{10,1... | collective-permute-start | bytes 2334728 | tf_op jit(solution)/shard_map/ppermute | solution.py:422
  46.5 0.8 copy-start
  46.5 1.1 %copy-start.1 = (bf16[5,152,512]{2,1,0:T(8,128)(2,1)}, bf16[5,152,512]{2,1,0:T(8,128)(2,1)S(1)}, u32[]{:S(2)}) copy-start(bf16[5,152,512]{2,1,0:T(8,128)(2,1)S(1)} %collective-permute-done.1.high_hbm) | copy-start | bytes 2334724

commit v4 on v3

--- a/solution.py
+++ b/solution.py
@@ -17,7 +17,7 @@
 ROW = 2 * LANES
 BAND = 512
 BLOCK = 256
-GROUP = 32
+GROUP = 8
 FETCH = 1024
 KINDS = 4
 SOUND_SPEED = 1.0
@@ -99,7 +99,7 @@
         pieces = []
         for v in range(variables):
             projected = jnp.dot(
-                proj_ref[kind], precursor_ref[v], preferred_element_type=jnp.float32
+                proj_ref[:, kind, :], precursor_ref[v], preferred_element_type=jnp.float32
             )
             pieces.append(jnp.concatenate([projected, gap], axis=0).astype(jnp.bfloat16))
         table = jnp.concatenate(pieces + [pad], axis=0)
@@ -129,7 +129,7 @@
             jax.ShapeDtypeStruct((nodes, FACES * TIGHT), jnp.bfloat16),
         ],
         compiler_params=pltpu.CompilerParams(vmem_limit_bytes=60 << 20),
-    )(mortar_send, precursor, mortar_proj, lift)
+    )(mortar_send, precursor, mortar_proj.transpose(1, 0, 2), lift)
 
 
 def volume_kernel(_, sol_ref, wind_ref, pick_ref, operator_ref, volume_ref, speed_ref):
@@ -255,7 +255,6 @@
             coupled.append(fetched.T)
             speed = speed_ref[face * SLOT : (face + 1) * SLOT, inner].astype(jnp.float32)[:TIGHT]
             coefficient.append(0.5 * (speed - jnp.abs(speed) - SOUND_SPEED))
-            emit(groups, 3)
         for v in range(variables):
             inside = jnp.dot(
                 pick_tight_ref[...], sol[v, :, block], preferred_element_type=jnp.float32
@@ -265,7 +264,7 @@
                 beyond = coupled[face][v * SLOT : (v + 1) * SLOT].astype(jnp.float32)[:TIGHT]
                 tight = slice(face * TIGHT, (face + 1) * TIGHT)
                 pieces.append((inside[tight] - beyond) * coefficient[face])
-                emit(groups, 1)
+                emit(groups, 7)
             surface = jnp.concatenate(pieces, axis=0).astype(jnp.bfloat16)
             total = jnp.dot(weight_ref[...], surface, preferred_element_type=jnp.float32)
             out_ref[v, :, inner] = (
@@ -319,7 +318,7 @@
                 )
                 return carry
 
-            lax.fori_loop(0, FETCH // BLOCK, build_own, 0, unroll=2)
+            lax.fori_loop(0, FETCH // BLOCK, build_own, 0, unroll=4)
         low_copy.wait()
         high_copy.wait()
         for side, first in ((0, 0), (1, (BAND + own) // BLOCK)):

time: 94.6 us -> 86.1 us (0.910)
  Pallas kernels: 70.8 us -> 63.4 us
  local copies, waits for them, and re-layouts: 3.27 us -> 1.74 us
    pallas_call x1, Pallas kernels: 46.6 us -> 39.4 us  [section_rate(): pl.pallas_call(rate_kernel, grid=(own // width,), in_specs=[anywhere, pl....]
    unnamed x7 -> x6, local copies, waits for them, and re-layouts: 2.58 us -> 1.05 us
  transfers between devices with their start and end apart: 3 -> 3, of which waited for: 0 -> 0; matrix products, arithmetic and copies ran while one was open for 1% -> 1% of each run, Pallas kernels for 22% -> 24%
where the time goes in v4:
time: 86.1 us; the launch traced here: 85.7 us
  Pallas kernels  63.4 us (74%)
  starting transfers between devices  20.2 us (23%)
  local copies, waits for them, and re-layouts  1.74 us (2%)
    pallas_call x1, Pallas kernels, section_rate(): pl.pallas_call(rate_kernel, grid=(own // width,), in_specs=[anywhere, pl....  39.4 us
    pallas_call x1, Pallas kernels, volume_terms(): pl.pallas_call(volume_kernel, grid=(own // width,), in_specs=[pl.BlockSpe...  17.5 us
    all_to_all x1, starting transfers between devices, local(): lax.all_to_all(sent, 'elem', split_axis=0, concat_axis=0, tiled=True)  10.5 us
    ppermute x1, starting transfers between devices, local(): high = lax.ppermute(first, 'elem', [(i + 1, i) for i in range(count - 1)])  7.62 us
    pallas_call x1, Pallas kernels, band_nodes(): pl.pallas_call(band_kernel, grid=(1,), in_specs=[pl.BlockSpec(memory_spac...  3.36 us
    pallas_call x1, Pallas kernels, mortar_rows(): pl.pallas_call(mortar_kernel, in_specs=[whole] * 4, out_shape=[jax.ShapeD...  3.24 us
    ppermute x1, starting transfers between devices, local(): low = lax.ppermute(last, 'elem', [(i, i + 1) for i in range(count - 1)])  2.1 us
  transfers between devices with their start and end apart: 3, of which 0 were waited for; matrix products, arithmetic and copies ran while one was open for 1% of the time, Pallas kernels for 24%

profile of v4, /device:TPU:6, one launch (start us, length us, event | category | flops | bytes accessed | tf_op | source)
XLA Modules:
  0.0 85.7 jit_solution(2871911620848189240)
XLA Ops:
  0.0 3.2 %shard_map.145 = (bf16[1024,256]{1,0:T(8,128)(2,1)}, bf16[216,240]{1,0:T(8,128)(2,1)}) custom-call(s32[1,2,1024]{2,1,0:T(2,128)} %send_ref.1, bf16[5,216,256]{2,1,0:T(8,128)(2,1)} %precursor_ref.1, bf16[36,4,216]{2,1,0:T(4,128)(2,1)} %bitcast.6, bf16[216,216]{1,0:T(8,128)(2,1)} %lift_ref.1), custom_call_target="tpu_custom_call" | custom-call | tf_op jit(solution)/shard_map/pallas_call | solution.py:124
  3.2 10.5 %all-to-all-start = ((bf16[128,8,256]{2,1,0:T(8,128)(2,1)}), bf16[128,8,256]{2,1,0:T(8,128)(2,1)S(1)}, u32[]{:S(2)}, u32[]{:S(2)}) async-start(bf16[128,8,256]{2,1,0:T(8,128)(2,1)} %bitcast.5), calls=%async_computation | async-start | bytes 1048576 | tf_op jit(solution)/shard_map/all_to_all | solution.py:419
  13.7 0.0 copy-start.2
  13.8 3.4 %shard_map.146 = (bf16[5,152,512]{2,1,0:T(8,128)(2,1)}, bf16[5,152,512]{2,1,0:T(8,128)(2,1)}) custom-call(bf16[1024,256]{1,0:T(8,128)(2,1)} %get-tuple-element.11._, bf16[152,216]{1,0:T(8,128)(2,1)} %constant.12.clone.pick_ref, bf16[5,216,4096]{2,1,0:T(8,128)(2,1)} %sol_hbm.1, bf16[5,216,4096]{2,1,0:T(8,128)(2,1)} %sol_hbm.1), custom_call_target="tpu_custom_call" | custom-call | tf_op jit(solution)/shard_map/pallas_call | solution.py:73
  17.1 7.6 %collective-permute-start.1 = (bf16[5,152,512]{2,1,0:T(8,128)(2,1)}, bf16[5,152,512]{2,1,0:T(8,128)(2,1)S(1)}, u32[]{:S(2)}, u32[]{:S(2)}) collective-permute-start(bf16[5,152,512]{2,1,0:T(8,128)(2,1)} %get-tuple-element.13), channel_id=1, source_target_pairs={{1,0},{2,1},{3,2},{4,3},{5,4},{6,5},{7,6},{8,7},{9,8},{10,9},{11,1... | collective-permute-start | bytes 2334728 | tf_op jit(solution)/shard_map/ppermute | solution.py:422
  24.7 2.1 %collective-permute-start = (bf16[5,152,512]{2,1,0:T(8,128)(2,1)}, bf16[5,152,512]{2,1,0:T(8,128)(2,1)}, u32[]{:S(2)}, u32[]{:S(2)}) collective-permute-start(bf16[5,152,512]{2,1,0:T(8,128)(2,1)} %get-tuple-element.12._), channel_id=1, source_target_pairs={{0,1},{1,2},{2,3},{3,4},{4,5},{5,6},{6,7},{7,8},{8,9},{9,10},{10,1... | collective-permute-start | bytes 2334728 | tf_op jit(solution)/shard_map/ppermute | solution.py:421
  26.9 0.0 copy-done.2
  26.9 0.1 add_multiply_fusion
  27.0 0.7 reshape.9.index_hbm
  27.6 17.5 %shard_map.147 = (f32[5,216,4096]{2,1,0:T(8,128)}, bf16[288,4096]{1,0:T(8,128)(2,1)}) custom-call(bf16[5,152,512]{2,1,0:T(8,128)(2,1)} %get-tuple-element.12._, bf16[5,216,4096]{2,1,0:T(8,128)(2,1)} %sol_hbm.1, bf16[3,216,4096]{2,1,0:T(8,128)(2,1)} %wind_ref.1, bf16[288,216]{1,0:T(8,128)(2,1)} %constant.13.clone.pick_ref, bf16[3,216,216]{2,1,0:T(8,128)(2,1)} %operator_ref.1), custom_call_target="tpu_custom_call" | custom-call | flops 5733089280 | bytes 35389440 | tf_op jit(solution)/shard_map/pallas_call | solution.py:157
  45.1 0.0 all-to-all-done
  45.1 0.0 copy-start
  45.1 0.0 collective-permute-done.1.high_hbm
  45.1 0.0 copy-start.1
  45.1 0.0 collective-permute-done.low_hbm
  45.2 0.8 copy-done
  45.9 0.3 copy-done.1
  46.2 39.4 %shard_map.148 = bf16[5,216,4096]{2,1,0:T(8,128)(2,1)} custom-call(s32[24576]{0:T(1024)} %reshape.9.index_hbm, s32[3,512]{1,0:T(4,128)} %fringe_ref.1, bf16[5,152,512]{2,1,0:T(8,128)(2,1)} %collective-permute-done.low_hbm, bf16[5,152,512]{2,1,0:T(8,128)(2,1)} %copy-done.1, bf16[5,216,4096]{2,1,0:T(8,128)(2,1)} %sol_hbm.1, ...), custom_call_target="tpu_custom_call" | custom-call | tf_op jit(solution)/shard_map/pallas_call | solution.py:357
  (1 shorter events, 0.0 us)
Async XLA Ops:
  3.2 41.9 %all-to-all-start = ((bf16[128,8,256]{2,1,0:T(8,128)(2,1)}), bf16[128,8,256]{2,1,0:T(8,128)(2,1)S(1)}, u32[]{:S(2)}, u32[]{:S(2)}) async-start(bf16[128,8,256]{2,1,0:T(8,128)(2,1)} %bitcast.5), calls=%async_computation | async-start | bytes 1048576 | tf_op jit(solution)/shard_map/all_to_all | solution.py:419
  13.7 13.1 %copy-start.2 = (s32[6,4096]{1,0:T(8,128)S(1)}, s32[6,4096]{1,0:T(8,128)}, u32[]{:S(2)}) copy-start(s32[6,4096]{1,0:T(8,128)} %param.18) | copy-start | bytes 294916
  17.1 28.0 %collective-permute-start.1 = (bf16[5,152,512]{2,1,0:T(8,128)(2,1)}, bf16[5,152,512]{2,1,0:T(8,128)(2,1)S(1)}, u32[]{:S(2)}, u32[]{:S(2)}) collective-permute-start(bf16[5,152,512]{2,1,0:T(8,128)(2,1)} %get-tuple-element.13), channel_id=1, source_target_pairs={{1,0},{2,1},{3,2},{4,3},{5,4},{6,5},{7,6},{8,7},{9,8},{10,9},{11,1... | collective-permute-start | bytes 2334728 | tf_op jit(solution)/shard_map/ppermute | solution.py:422
  24.7 20.4 %collective-permute-start = (bf16[5,152,512]{2,1,0:T(8,128)(2,1)}, bf16[5,152,512]{2,1,0:T(8,128)(2,1)}, u32[]{:S(2)}, u32[]{:S(2)}) collective-permute-start(bf16[5,152,512]{2,1,0:T(8,128)(2,1)} %get-tuple-element.12._), channel_id=1, source_target_pairs={{0,1},{1,2},{2,3},{3,4},{4,5},{5,6},{6,7},{7,8},{8,9},{9,10},{10,1... | collective-permute-start | bytes 2334728 | tf_op jit(solution)/shard_map/ppermute | solution.py:421
  45.1 0.8 copy-start
  45.1 1.1 %copy-start.1 = (bf16[5,152,512]{2,1,0:T(8,128)(2,1)}, bf16[5,152,512]{2,1,0:T(8,128)(2,1)S(1)}, u32[]{:S(2)}) copy-start(bf16[5,152,512]{2,1,0:T(8,128)(2,1)S(1)} %collective-permute-done.1.high_hbm) | copy-start | bytes 2334724
